TPU v7x, 32 devices: a whole 2x2x4 slice. The times are simulated.
32 devices in a mesh: ctx: 8 (over z, y), wa: 4 (over x, core).
Axes of the slice: x: 2, y: 2, z: 4, core: 2. Of those that a mesh axis runs over, the one named last changes fastest.
Arguments:
- inputs: float32 [2048, 2, 768], P('ctx'), may hold values from -6 to 6
- upstream: float32 [2048, 2, 768], P('ctx'), may hold values from -6 to 6
- gain_attn: float32 [768], replicated, may hold values from 0.5 to 1.5
- w_query: bfloat16 [768, 768], P(None, 'wa'), may hold values from -0.078125 to 0.078125
- w_key: bfloat16 [768, 768], P(None, 'wa'), may hold values from -0.078125 to 0.078125
- w_value: bfloat16 [768, 768], P(None, 'wa'), may hold values from -0.21875 to 0.21875
- w_proj: bfloat16 [768, 768], P('wa'), may hold values from -6 to 6
- rel_bias: float32 [32, 12], P(None, 'wa'), may hold values from -4 to 4
- gain_ffn: float32 [768], replicated, may hold values from 0.5 to 1.5
- w_router: bfloat16 [768, 8], replicated, may hold values from -0.15625 to 0.15625
- w_expin: bfloat16 [8, 768, 3072], P('ctx', None, 'wa'), may hold values from -0.21875 to 0.21875
- w_expout: bfloat16 [8, 3072, 768], P('ctx', 'wa'), may hold values from -1.5 to 1.5
- routes: int32 [2048, 2, 1], P('ctx'), may hold values from 0 to 7; in each aligned block of 512 rows (0 to 511, 512 to 1023, ..., all dimensions but the last counted through in order) at most 128 rows name the same one
- bucket_table: int32 [4095], replicated, may hold values from 0 to 31, as said below
Outputs:
- output: float32 [2048, 2, 768], P('ctx')
- grad_inputs: float32 [2048, 2, 768], P('ctx')
- grad_gain_attn: float32 [768], replicated
- grad_w_query: float32 [768, 768], P(None, 'wa')
- grad_w_key: float32 [768, 768], P(None, 'wa')
- grad_w_value: float32 [768, 768], P(None, 'wa')
- grad_w_proj: float32 [768, 768], P('wa')
- grad_rel_bias: float32 [32, 12], P(None, 'wa')
- grad_gain_ffn: float32 [768], replicated
- grad_w_router: float32 [768, 8], replicated
- grad_w_expin: float32 [8, 768, 3072], P('ctx', None, 'wa')
- grad_w_expout: float32 [8, 3072, 768], P('ctx', 'wa')
Inputs may be any that keep to these rules, and one draw needn't show every extreme that they name: `routes`: among the 512 tokens of one ctx device (positions of its block, then sequences) at most 128 have the same route, and some route has exactly 128 of them. `bucket_table`: entry r + 2047 is the bucket of a key r positions after its query (before it for negative r); it is 0 at r = 0 and 31 at r = 2047.
All inputs are finite; a program needn't handle non-finite values.
Results may differ from a plain program's by a relative error of at most 0.024.
Values may be sent and summed in bfloat16 or wider, within the bound.
A program may use at most 128 MiB of HBM per device.

v0:
```python
import jax
import jax.numpy as jnp
from jax import lax
from jax.sharding import PartitionSpec as P

eps = 1e-06
neg_large = -1e30
highest = lax.Precision.HIGHEST


def passed_along(value, axis, steps):
    count = lax.axis_size(axis)
    pairs = [(source, (source + steps) % count) for source in range(count)]
    return lax.ppermute(value, axis, pairs)


def gelu_tanh(values):
    return jax.nn.gelu(values, approximate=True)


def rms_forward(flat_rows, gain):
    scale = lax.rsqrt(jnp.mean(flat_rows * flat_rows, axis=-1, keepdims=True) + eps)
    return (flat_rows * scale * gain, scale)


def rms_backward(flat_rows, scale, gain, grad_out):
    weighted = grad_out * gain
    inner_mean = jnp.mean(weighted * flat_rows, axis=-1, keepdims=True)
    grad_rows = scale * weighted - flat_rows * scale * scale * scale * inner_mean
    grad_gain = jnp.sum(grad_out * flat_rows * scale, axis=0)
    return (grad_rows, grad_gain)


def offset_bias(table, rel_bias, window_base, query_len, key_len):
    line_len = query_len + key_len - 1
    window = lax.dynamic_slice_in_dim(table, window_base, line_len)
    bucket_ids = jnp.arange(rel_bias.shape[0], dtype=jnp.int32)
    chosen = (window[:, None] == bucket_ids[None, :]).astype(jnp.float32)
    line = jnp.transpose(jnp.dot(chosen, rel_bias, precision=highest))
    head_count = line.shape[0]
    padded = jnp.pad(line, ((0, 0), (0, 1)))
    tiled = jnp.tile(padded, (1, query_len))[:, : query_len * line_len]
    skewed = tiled.reshape(head_count, query_len, line_len)
    return skewed[:, :, query_len - 1 : query_len - 1 + key_len]


def bias_grad(table, window_base, query_len, key_len, line, bucket_count):
    window = lax.dynamic_slice_in_dim(table, window_base, query_len + key_len - 1)
    bucket_ids = jnp.arange(bucket_count, dtype=jnp.int32)
    chosen = (window[:, None] == bucket_ids[None, :]).astype(jnp.float32)
    return jnp.einsum("jb,hj->bh", chosen, line, precision=highest)


def diagonal_sums(square):
    head_count, query_len, key_len = square.shape
    flipped = square[:, ::-1, :]
    padded = jnp.pad(flipped, ((0, 0), (0, 0), (0, query_len)))
    flat_view = padded.reshape(head_count, query_len * (key_len + query_len))
    flat_view = flat_view[:, : query_len * (key_len + query_len - 1)]
    return jnp.sum(flat_view.reshape(head_count, query_len, key_len + query_len - 1), axis=1)


def block_scores(query4, key_part, table, rel_bias, key_first, query_first, seq_len):
    query_len, seq_count, head_local, head_dim = query4.shape
    key_len = key_part.shape[0]
    key4 = key_part.reshape(key_len, seq_count, head_local, head_dim)
    raw_scores = jnp.einsum("qshd,kshd->shqk", query4, key4, preferred_element_type=jnp.float32)
    window_base = key_first - query_first - (query_len - 1) + seq_len - 1
    return raw_scores + offset_bias(table, rel_bias, window_base, query_len, key_len)[None]


def make_stats(query4, table, rel_bias, query_first, seq_len):

    def fold_stats(running, portion, first_row):
        total_len = portion.shape[0]
        key_width = 512

        def sub_block(number, current):
            row_top, row_mass = current
            part_keys = lax.dynamic_slice_in_dim(portion, number * key_width, key_width, 0)
            scores = block_scores(
                query4, part_keys, table, rel_bias, number * key_width, query_first, seq_len
            )
            new_top = jnp.maximum(row_top, jnp.max(scores, axis=-1, keepdims=True))
            row_mass = row_mass * jnp.exp(row_top - new_top) + jnp.sum(
                jnp.exp(scores - new_top), axis=-1, keepdims=True
            )
            return (new_top, row_mass)

        return lax.fori_loop(0, total_len // key_width, sub_block, running)

    return fold_stats


def make_values(query4, log_total, table, rel_bias, query_first, seq_len):

    def fold_values(running, portion, first_row):
        key_part, value_part = portion
        total_len = key_part.shape[0]
        key_width = 512

        def sub_block(number, accum):
            part_keys = lax.dynamic_slice_in_dim(key_part, number * key_width, key_width, 0)
            part_values = lax.dynamic_slice_in_dim(value_part, number * key_width, key_width, 0)
            scores = block_scores(
                query4, part_keys, table, rel_bias, number * key_width, query_first, seq_len
            )
            weights = jnp.exp(scores - log_total).astype(jnp.bfloat16)
            value4 = part_values.reshape(
                key_width, query4.shape[1], query4.shape[2], query4.shape[3]
            )
            return accum + jnp.einsum(
                "shqk,kshd->qshd", weights, value4, preferred_element_type=jnp.float32
            )

        return lax.fori_loop(0, total_len // key_width, sub_block, running)

    return fold_values


def block_backward(
    query4,
    grad4,
    log_total,
    delta,
    key_part,
    value_part,
    table,
    rel_bias,
    key_first,
    query_first,
    seq_len,
):
    block_len = query4.shape[0]
    scores = block_scores(query4, key_part, table, rel_bias, key_first, query_first, seq_len)
    weights = jnp.exp(scores - log_total)
    key4 = key_part.reshape(query4.shape)
    value4 = value_part.reshape(query4.shape)
    grad_weights = jnp.einsum("qshd,kshd->shqk", grad4, value4, preferred_element_type=jnp.float32)
    grad_scores = (weights * (grad_weights - delta)).astype(jnp.bfloat16)
    grad_query = jnp.einsum(
        "shqk,kshd->qshd", grad_scores, key4, preferred_element_type=jnp.float32
    )
    grad_keys = jnp.einsum(
        "shqk,qshd->kshd", grad_scores, query4, preferred_element_type=jnp.float32
    ).reshape(key_part.shape)
    grad_values = jnp.einsum(
        "shqk,qshd->kshd", weights.astype(jnp.bfloat16), grad4, preferred_element_type=jnp.float32
    ).reshape(key_part.shape)
    line = diagonal_sums(jnp.sum(grad_scores.astype(jnp.float32), axis=0))
    window_base = key_first - query_first - (block_len - 1) + seq_len - 1
    grad_bias = bias_grad(table, window_base, block_len, block_len, line, rel_bias.shape[0])
    return (grad_query, grad_keys, grad_values, grad_bias)


def rotate_backward(
    query4,
    grad4,
    log_total,
    delta,
    key_rows,
    value_rows,
    table,
    rel_bias,
    query_first,
    seq_len,
    my_index,
    ctx_size,
):
    block_len = query4.shape[0]
    zero_rows = jnp.zeros(key_rows.shape, jnp.float32)
    initial = (
        key_rows,
        value_rows,
        zero_rows,
        zero_rows,
        jnp.zeros(query4.shape, jnp.float32),
        jnp.zeros(rel_bias.shape, jnp.float32),
    )

    def rotate_turn(turn_index, state_now):
        key_part, value_part, grad_keys, grad_values, grad_query, grad_bias = state_now
        for parity in range(2):
            anchor = jnp.mod(my_index - 2 * turn_index - parity, ctx_size)
            key_first = anchor * block_len
            part_query, part_keys, part_values, part_bias = block_backward(
                query4,
                grad4,
                log_total,
                delta,
                key_part,
                value_part,
                table,
                rel_bias,
                key_first,
                query_first,
                seq_len,
            )
            grad_query = grad_query + part_query
            grad_keys = grad_keys + part_keys
            grad_values = grad_values + part_values
            grad_bias = grad_bias + part_bias
            key_part, value_part = passed_along((key_part, value_part), "ctx", 1)
            grad_keys, grad_values = (
                passed_along(grad_keys.astype(jnp.bfloat16), "ctx", 1).astype(grad_keys.dtype),
                passed_along(grad_values.astype(jnp.bfloat16), "ctx", 1).astype(grad_values.dtype),
            )
        return (key_part, value_part, grad_keys, grad_values, grad_query, grad_bias)

    final = lax.fori_loop(0, ctx_size // 2, rotate_turn, initial)
    return (final[4], final[2], final[3], final[5])


def body(
    inputs,
    upstream,
    gain_attn,
    w_query,
    w_key,
    w_value,
    w_proj,
    rel_bias,
    gain_ffn,
    w_router,
    w_expin,
    w_expout,
    routes,
    bucket_table,
):
    block_len, seq_count, model_width = inputs.shape
    ctx_size = lax.axis_size("ctx")
    seq_len = block_len * ctx_size
    tok_count = block_len * seq_count
    head_local = rel_bias.shape[1]
    head_cols = w_query.shape[1]
    head_dim = head_cols // head_local
    expert_count = w_router.shape[1]
    capacity = 2 * tok_count // expert_count
    my_index = lax.axis_index("ctx")
    query_first = my_index * block_len
    shape4 = (block_len, seq_count, head_local, head_dim)
    flat_rows = inputs.reshape(tok_count, model_width)
    normed1, scale1 = rms_forward(flat_rows, gain_attn)
    normed1_low = normed1.astype(jnp.bfloat16)
    query_low = jnp.dot(normed1_low, w_query, preferred_element_type=jnp.float32).astype(
        jnp.bfloat16
    )
    key_low = jnp.dot(normed1_low, w_key, preferred_element_type=jnp.float32).astype(jnp.bfloat16)
    value_low = jnp.dot(normed1_low, w_value, preferred_element_type=jnp.float32).astype(
        jnp.bfloat16
    )
    query4 = query_low.reshape(shape4)
    key_rows = key_low.reshape(block_len, seq_count, head_cols)
    value_rows = value_low.reshape(block_len, seq_count, head_cols)
    stats_shape = (seq_count, head_local, block_len, 1)
    stats_init = (
        jnp.full(stats_shape, neg_large, jnp.float32),
        jnp.zeros(stats_shape, jnp.float32),
    )
    fold_stats = make_stats(query4, bucket_table, rel_bias, query_first, seq_len)
    value_init = jnp.zeros(shape4, jnp.float32)
    row_top, row_mass = fold_stats(
        stats_init, lax.all_gather(key_rows, "ctx", axis=0, tiled=True), jnp.int32(0)
    )
    log_total = row_top + jnp.log(row_mass)
    fold_values = make_values(query4, log_total, bucket_table, rel_bias, query_first, seq_len)
    attended = fold_values(
        value_init,
        (
            lax.all_gather(key_rows, "ctx", axis=0, tiled=True),
            lax.all_gather(value_rows, "ctx", axis=0, tiled=True),
        ),
        jnp.int32(0),
    )
    attended_low = attended.reshape(tok_count, head_cols).astype(jnp.bfloat16)
    attn_share = jnp.dot(attended_low, w_proj, preferred_element_type=jnp.float32)
    attn_out = lax.psum(attn_share.astype(jnp.bfloat16), "wa").astype(jnp.float32)
    hidden1 = flat_rows + attn_out
    normed2, scale2 = rms_forward(hidden1, gain_ffn)
    normed2_low = normed2.astype(jnp.bfloat16)
    logits = jnp.dot(normed2_low, w_router, preferred_element_type=jnp.float32)
    router_prob = jax.nn.softmax(logits, axis=-1)
    route_flat = routes.reshape(tok_count)
    expert_ids = jnp.arange(expert_count, dtype=jnp.int32)
    chosen = route_flat[:, None] == expert_ids[None, :]
    chosen_int = chosen.astype(jnp.int32)
    chosen_float = chosen.astype(jnp.float32)
    gate_value = jnp.sum(router_prob * chosen_float, axis=1)
    counts = jnp.cumsum(chosen_int, axis=0)
    slot_rank = jnp.sum((counts - 1) * chosen_int, axis=1)
    slot_index = route_flat * capacity + slot_rank
    slot_ids = jnp.arange(expert_count * capacity, dtype=jnp.int32)
    dispatch = (slot_ids[:, None] == slot_index[None, :]).astype(jnp.bfloat16)

    def send_slots(values_low):
        packed = jnp.dot(dispatch, values_low, preferred_element_type=jnp.float32).astype(
            jnp.bfloat16
        )
        return lax.all_to_all(
            packed.reshape(expert_count, capacity, model_width),
            "ctx",
            split_axis=0,
            concat_axis=1,
            tiled=True,
        )

    def unit_return(partial_rows):
        returned = lax.all_to_all(
            partial_rows.astype(jnp.bfloat16), "ctx", split_axis=1, concat_axis=0, tiled=True
        ).astype(partial_rows.dtype)
        summed_rows = lax.psum(returned.astype(jnp.bfloat16), "wa").astype(jnp.float32)
        return jnp.take(
            summed_rows.reshape(expert_count * capacity, model_width), slot_index, axis=0
        )

    received = send_slots(normed2_low)
    pre_act = jnp.einsum("erd,edf->erf", received, w_expin, preferred_element_type=jnp.float32)
    activated, gelu_back = jax.vjp(gelu_tanh, pre_act)
    activated_low = activated.astype(jnp.bfloat16)
    expert_part = jnp.einsum(
        "erf,efd->erd", activated_low, w_expout, preferred_element_type=jnp.float32
    )
    expert_out = unit_return(expert_part)
    output_rows = hidden1 + gate_value[:, None] * expert_out
    grad_rows = upstream.reshape(tok_count, model_width)
    grad_expert = (gate_value[:, None] * grad_rows).astype(jnp.bfloat16)
    grad_gate = jnp.sum(grad_rows * expert_out, axis=1)
    grad_received = send_slots(grad_expert)
    grad_wout = jnp.einsum(
        "erf,erd->efd", activated_low, grad_received, preferred_element_type=jnp.float32
    )
    grad_act = jnp.einsum(
        "erd,efd->erf", grad_received, w_expout, preferred_element_type=jnp.float32
    )
    grad_pre = gelu_back(grad_act)[0].astype(jnp.bfloat16)
    grad_win = jnp.einsum("erd,erf->edf", received, grad_pre, preferred_element_type=jnp.float32)
    grad_inpart = jnp.einsum("erf,edf->erd", grad_pre, w_expin, preferred_element_type=jnp.float32)
    grad_from_experts = unit_return(grad_inpart)
    grad_logits = router_prob * (chosen_float - gate_value[:, None]) * grad_gate[:, None]
    router_float = w_router.astype(jnp.float32)
    grad_normed2 = grad_from_experts + jnp.einsum(
        "te,de->td", grad_logits, router_float, precision=highest
    )
    grad_router = jnp.einsum(
        "td,te->de", normed2_low.astype(jnp.float32), grad_logits, precision=highest
    )
    grad_norm2_in, grad_gain2 = rms_backward(hidden1, scale2, gain_ffn, grad_normed2)
    grad_hidden1 = grad_rows + grad_norm2_in
    grad_attn_low = grad_hidden1.astype(jnp.bfloat16)
    grad_proj = jnp.einsum(
        "tk,td->kd", attended_low, grad_attn_low, preferred_element_type=jnp.float32
    )
    grad_attended = jnp.einsum(
        "td,kd->tk", grad_attn_low, w_proj, preferred_element_type=jnp.float32
    ).astype(jnp.bfloat16)
    grad4 = grad_attended.reshape(shape4)
    delta = jnp.transpose(jnp.sum(grad4.astype(jnp.float32) * attended, axis=-1), (1, 2, 0))[
        ..., None
    ]
    grad_query, grad_keys, grad_values, grad_bias = rotate_backward(
        query4,
        grad4,
        log_total,
        delta,
        key_rows,
        value_rows,
        bucket_table,
        rel_bias,
        query_first,
        seq_len,
        my_index,
        ctx_size,
    )
    grad_query_low = grad_query.reshape(tok_count, head_cols).astype(jnp.bfloat16)
    grad_key_low = grad_keys.reshape(tok_count, head_cols).astype(jnp.bfloat16)
    grad_value_low = grad_values.reshape(tok_count, head_cols).astype(jnp.bfloat16)
    grad_wq = jnp.einsum(
        "tc,tk->ck", normed1_low, grad_query_low, preferred_element_type=jnp.float32
    )
    grad_wk = jnp.einsum("tc,tk->ck", normed1_low, grad_key_low, preferred_element_type=jnp.float32)
    grad_wv = jnp.einsum(
        "tc,tk->ck", normed1_low, grad_value_low, preferred_element_type=jnp.float32
    )
    grad_normed1_part = (
        jnp.einsum("tk,ck->tc", grad_query_low, w_query, preferred_element_type=jnp.float32)
        + jnp.einsum("tk,ck->tc", grad_key_low, w_key, preferred_element_type=jnp.float32)
        + jnp.einsum("tk,ck->tc", grad_value_low, w_value, preferred_element_type=jnp.float32)
    )
    grad_normed1 = lax.psum(grad_normed1_part.astype(jnp.bfloat16), "wa").astype(jnp.float32)
    grad_norm1_in, grad_gain1 = rms_backward(flat_rows, scale1, gain_attn, grad_normed1)
    grad_inputs = grad_hidden1 + grad_norm1_in
    summed = (
        lax.psum(grad_wq.astype(jnp.bfloat16), "ctx").astype(jnp.float32),
        lax.psum(grad_wk.astype(jnp.bfloat16), "ctx").astype(jnp.float32),
        lax.psum(grad_wv.astype(jnp.bfloat16), "ctx").astype(jnp.float32),
        lax.psum(grad_proj.astype(jnp.bfloat16), "ctx").astype(jnp.float32),
        lax.psum(grad_bias.astype(jnp.bfloat16), "ctx").astype(jnp.float32),
        lax.psum(grad_router.astype(jnp.bfloat16), "ctx").astype(jnp.float32),
        lax.psum(grad_gain1.astype(jnp.bfloat16), "ctx").astype(jnp.float32),
        lax.psum(grad_gain2.astype(jnp.bfloat16), "ctx").astype(jnp.float32),
    )
    return (
        output_rows.reshape(inputs.shape),
        grad_inputs.reshape(inputs.shape),
        summed[6],
        summed[0],
        summed[1],
        summed[2],
        summed[3],
        summed[4],
        summed[7],
        summed[5],
        grad_win,
        grad_wout,
    )


def solution(mesh):
    in_specs = (
        P("ctx", None, None),
        P("ctx", None, None),
        P(),
        P(None, "wa"),
        P(None, "wa"),
        P(None, "wa"),
        P("wa", None),
        P(None, "wa"),
        P(),
        P(),
        P("ctx", None, "wa"),
        P("ctx", "wa", None),
        P("ctx", None, None),
        P(),
    )
    out_specs = (
        P("ctx", None, None),
        P("ctx", None, None),
        P(),
        P(None, "wa"),
        P(None, "wa"),
        P(None, "wa"),
        P("wa", None),
        P(None, "wa"),
        P(),
        P(),
        P("ctx", None, "wa"),
        P("ctx", "wa", None),
    )
    return jax.shard_map(body, mesh=mesh, in_specs=in_specs, out_specs=out_specs, check_vma=False)
```

profile of v0, /device:TPU:0, one launch (start us, length us, event | category | flops | bytes accessed | tf_op | source)
XLA Modules:
  0.0 953.1 jit_solution(3171041156745496191)
XLA Ops:
  23.6 42.2 %all-gather.5.cloned.1.call-done = bf16[2048,2,192]{0,2,1:T(8,128)(2,1)} async-done(((bf16[256,2,192]{0,2,1:T(8,128)(2,1)}), bf16[2048,2,192]{0,2,1:T(8,128)(2,1)}) %all-gather.5.cloned.1.call-update) | async-done | bytes 1572880 | tf_op jit(solution)/shard_map/all_gather | solution.py:270
  65.8 79.8 %while.67 = (s32[]{:T(128)}, f32[2,3,256,1]{2,1,0,3:T(4,128)S(1)}, f32[2,3,256,1]{2,1,0,3:T(4,128)S(1)}, bf16[2048,2,192]{0,2,1:T(8,128)(2,1)}, bf16[256,2,3,64]...) while((s32[]{:T(128)}, f32[2,3,256,1]{2,1,0,3:T(4,128)S(1)}, ...), condition=%wide.region_4.5_spmd.clone, body=%wide.region_1.4_spmd.clone.sunk | while | flops 105511272 | bytes 34520712 | solution.py:90
  71.4 5.0 reshape.612
  91.4 5.1 reshape.612
  147.0 76.6 %while.68 = (s32[]{:T(128)}, f32[256,2,3,64]{0,3,2,1:T(8,128)}, bf16[2048,2,192]{0,2,1:T(8,128)(2,1)}, bf16[2048,2,192]{0,2,1:T(8,128)(2,1)}, bf16[256,2,3,64]{0...) while((s32[]{:T(128)}, f32[256,2,3,64]{0,3,2,1:T(8,128)}, ...), condition=%wide.region_6.7_spmd.clone, body=%wide.region_5.6_spmd.clone.sunk | while | flops 204790640 | bytes 30121644 | solution.py:116
  228.9 31.8 %all-reduce.14.cloned.1.call-done = bf16[512,768]{1,0:T(8,128)(2,1)} async-done(((bf16[512,768]{1,0:T(8,128)(2,1)}), bf16[512,768]{1,0:T(8,128)(2,1)}) %all-reduce.14.cloned.1.call-update) | async-done | bytes 786448 | tf_op jit(solution)/shard_map/psum | solution.py:277
  265.0 5.5 all-to-all-start
  277.6 29.3 %all-to-all-done = bf16[8,128,768]{2,1,0:T(8,128)(2,1)} async-done(((bf16[8,128,768]{2,1,0:T(8,128)(2,1)}), bf16[8,128,768]{2,1,0:T(8,128)(2,1)}, u32[]{:S(2)}, u32[]{:S(2)}) %all-to-all-start) | async-done | bytes 1572896 | tf_op jit(solution)/shard_map/all_to_all | solution.py:299
  314.9 32.7 %all-to-all-done.2 = bf16[8,128,768]{2,1,0:T(8,128)(2,1)S(1)} async-done(((bf16[8,128,768]{2,1,0:T(8,128)(2,1)}), bf16[8,128,768]{2,1,0:T(8,128)(2,1)S(1)}, u32[]{:S(2)}, u32[]{:S(2)}) %all-to-all-start.2) | async-done | bytes 1572896 | tf_op jit(solution)/shard_map/all_to_all | solution.py:299
  347.6 5.8 fusion.29
  359.4 11.4 %reduce.3 = bf16[1024,768]{1,0:T(8,128)(2,1)S(1)} reduce(bf16[1024,1,768]{2,1,0:T(2,128)(2,1)} %bitcast.359, bf16[]{:T(256)} %broadcast.290), dimensions={1}, to_apply=%bitcast.212.reduce_sub_computation | reduce | bytes 3145730
  385.1 11.6 %reduce.4 = bf16[1024,768]{1,0:T(8,128)(2,1)S(1)} reduce(bf16[1024,1,768]{2,1,0:T(2,128)(2,1)} %bitcast.360, bf16[]{:T(256)} %broadcast.290), dimensions={1}, to_apply=%bitcast.213.reduce_sub_computation | reduce | bytes 3145730
  398.5 15.2 %all-to-all-done.3 = bf16[8,2,49152]{2,1,0:T(2,128)(2,1)} async-done(((bf16[8,2,49152]{2,1,0:T(2,128)(2,1)}), bf16[8,2,49152]{2,1,0:T(2,128)(2,1)}, u32[]{:S(2)}, u32[]{:S(2)}) %all-to-all-start.3) | async-done | bytes 1572896 | tf_op jit(solution)/shard_map/all_to_all | solution.py:308
  417.4 6.3 reshape.605
  423.7 30.8 %all-to-all-done.1 = bf16[8,2,49152]{2,1,0:T(2,128)(2,1)S(1)} async-done(((bf16[8,2,49152]{2,1,0:T(2,128)(2,1)}), bf16[8,2,49152]{2,1,0:T(2,128)(2,1)S(1)}, u32[]{:S(2)}, u32[]{:S(2)}) %all-to-all-start.1) | async-done | bytes 1572896 | tf_op jit(solution)/shard_map/all_to_all | solution.py:308
  468.3 5.1 convolution_bitcast_fusion.6
  473.4 57.5 %all-reduce.20.cloned.1.call-done = (bf16[1024,768]{1,0:T(8,128)(2,1)}, bf16[1024,768]{1,0:T(8,128)(2,1)}) async-done(((bf16[1024,768]{1,0:T(8,128)(2,1)}, bf16[1024,768]{1,0:T(8,128)(2,1)}), (bf16[1024,768]{1,0:T(8,128)(2,1)}, bf16[1024,768]{1,0:T(8,128)(2,1)})) %all-reduce.20.cloned.1.call-update) | async-done | bytes 3145744 | tf_op jit(solution)/shard_map/psum | solution.py:311
  536.2 5.1 gather_fusion
  541.3 5.2 gather_fusion.1
  555.9 254.8 %while.69 = (s32[]{:T(128)}, bf16[256,2,192]{0,2,1:T(8,128)(2,1)S(1)}, bf16[256,2,192]{0,2,1:T(8,128)(2,1)}, f32[256,2,192]{0,2,1:T(8,128)}, f32[256,2,192]{0,2,...) while((s32[]{:T(128)}, ...), condition=%wide.region_25.27_spmd.clone, body=%wide.region_20.0_spmd.clone.sunk | while | flops 514088128 | bytes 101905640 | solution.py:210
  800.2 5.1 collective-permute-start.3
  834.8 20.1 %all-reduce.16.cloned.1.call-done = bf16[512,768]{1,0:T(8,128)(2,1)} async-done(((bf16[512,768]{1,0:T(8,128)(2,1)}), bf16[512,768]{1,0:T(8,128)(2,1)}) %all-reduce.16.cloned.1.call-update) | async-done | bytes 786448 | tf_op jit(solution)/shard_map/psum | solution.py:389
  862.8 37.5 %all-reduce.6 = (bf16[768]{0:T(1024)(128)(2,1)S(1)}, bf16[32,3]{0,1:T(4,128)(2,1)S(1)}, bf16[768]{0:T(1024)(128)(2,1)S(1)}, bf16[768,8]{0,1:T(8,128)(2,1)S(1)}) all-reduce(bf16[768]{0:T(1024)(128)(2,1)S(1)} %get-tuple-element.1361, bf16[32,3]{0,1:T(4,128)(2,1)S(1)} %convert_element_type.457, ...), channel_id=1, replica_groups=mesh['ctx'=8,'wa'=4] {'ctx'}, use_global_device_ids=true, to_apply=%region_29.31 | all-reduce | flops 7776 | bytes 31104 | tf_op jit(solution)/shard_map/psum | solution.py:399
  902.7 37.8 %all-reduce.18.cloned.1.call-done = (bf16[768,192]{0,1:T(8,128)(2,1)}, bf16[768,192]{0,1:T(8,128)(2,1)}, bf16[768,192]{0,1:T(8,128)(2,1)}, bf16[192,768]{1,0:T(8,128)(2,1)}) async-done(((bf16[768,192]{0,1:T(8,128)(2,1)}, bf16[768,192]{0,1:T(8,128)(2,1)}, bf16[768,192]{0,1:T(8,128)(2,1)}, bf16[192,768]{1,0:T(8,128)(2,1)}), (bf16[768,192]{0,1:T(8,128)(2,1)}, bf16[768,192]{0,1:T(8,128)(2,1)}, ...) | async-done | bytes 1179664 | tf_op jit(solution)/shard_map/psum | solution.py:393
  (688 shorter events, 529.5 us)
Async XLA Ops:
  7.2 58.6 %all-gather.5.cloned.1.call-start = ((), (), s32[]{:S(2)}) async-start(), calls=%async_computation.5 | async-start | bytes 1769472 | tf_op jit(solution)/shard_map/all_gather | solution.py:270
  17.6 129.3 %all-gather.3.cloned.1.call-start = ((), (), s32[]{:S(2)}) async-start(), calls=%async_computation.4 | async-start | bytes 1769472 | tf_op jit(solution)/shard_map/all_gather | solution.py:271
  19.3 241.4 %all-reduce.14.cloned.1.call-start = ((), (), s32[]{:S(2)}) async-start(), calls=%async_computation.6 | async-start | bytes 1572864 | tf_op jit(solution)/shard_map/psum | solution.py:277
  265.0 41.8 %all-to-all-start = ((bf16[8,128,768]{2,1,0:T(8,128)(2,1)}), bf16[8,128,768]{2,1,0:T(8,128)(2,1)}, u32[]{:S(2)}, u32[]{:S(2)}) async-start(bf16[8,128,768]{2,1,0:T(8,128)(2,1)} %bitcast.2), calls=%async_computation | async-start | bytes 3145728 | tf_op jit(solution)/shard_map/all_to_all | solution.py:299
  306.9 40.7 %all-to-all-start.2 = ((bf16[8,128,768]{2,1,0:T(8,128)(2,1)}), bf16[8,128,768]{2,1,0:T(8,128)(2,1)S(1)}, u32[]{:S(2)}, u32[]{:S(2)}) async-start(bf16[8,128,768]{2,1,0:T(8,128)(2,1)} %bitcast.368), calls=%async_computation.2 | async-start | bytes 3145728 | tf_op jit(solution)/shard_map/all_to_all | solution.py:299
  372.6 41.1 %all-to-all-start.3 = ((bf16[8,2,49152]{2,1,0:T(2,128)(2,1)}), bf16[8,2,49152]{2,1,0:T(2,128)(2,1)}, u32[]{:S(2)}, u32[]{:S(2)}) async-start(bf16[8,2,49152]{2,1,0:T(2,128)(2,1)} %reshape.604), calls=%async_computation.3 | async-start | bytes 3145728 | tf_op jit(solution)/shard_map/all_to_all | solution.py:308
  413.7 40.8 %all-to-all-start.1 = ((bf16[8,2,49152]{2,1,0:T(2,128)(2,1)}), bf16[8,2,49152]{2,1,0:T(2,128)(2,1)S(1)}, u32[]{:S(2)}, u32[]{:S(2)}) async-start(bf16[8,2,49152]{2,1,0:T(2,128)(2,1)} %reshape.602), calls=%async_computation.1 | async-start | bytes 3145728 | tf_op jit(solution)/shard_map/all_to_all | solution.py:308
  417.3 113.6 %all-reduce.20.cloned.1.call-start = ((), (), s32[]{:S(2)}) async-start(), calls=%async_computation.9 | async-start | bytes 6291456 | tf_op jit(solution)/shard_map/psum | solution.py:311
  463.5 391.3 %all-reduce.16.cloned.1.call-start = ((), (), s32[]{:S(2)}) async-start(), calls=%async_computation.7 | async-start | bytes 1572864 | tf_op jit(solution)/shard_map/psum | solution.py:389
  556.1 35.2 %collective-permute-start = (bf16[256,2,192]{0,2,1:T(8,128)(2,1)S(1)}, bf16[256,2,192]{0,2,1:T(8,128)(2,1)}, u32[]{:S(2)}, u32[]{:S(2)}) collective-permute-start(bf16[256,2,192]{0,2,1:T(8,128)(2,1)S(1)} %get-tuple-element.1792), channel_id=1, source_target_pairs={{0,4},{4,8},{8,12},{12,16},{16,20},{20,24},{24,28},{28,0},{1,5},{5... | collective-permute-start | bytes 589832 | tf_op jit(solution)/shard_map/while/body/eval_jaxpr/ppermute | solution.py:14
  557.6 35.1 %collective-permute-start.2 = (bf16[256,2,192]{0,2,1:T(8,128)(2,1)}, bf16[256,2,192]{0,2,1:T(8,128)(2,1)}, u32[]{:S(2)}, u32[]{:S(2)}) collective-permute-start(bf16[256,2,192]{0,2,1:T(8,128)(2,1)} %get-tuple-element.1793), channel_id=1, source_target_pairs={{0,4},{4,8},{8,12},{12,16},{16,20},{20,24},{24,28},{28,0},{1,5},{5... | collective-permute-start | bytes 589832 | tf_op jit(solution)/shard_map/while/body/eval_jaxpr/ppermute | solution.py:14
  571.4 23.0 %collective-permute-start.4 = (bf16[256,2,192]{0,2,1:T(8,128)(2,1)}, bf16[256,2,192]{0,2,1:T(8,128)(2,1)}, u32[]{:S(2)}, u32[]{:S(2)}) collective-permute-start(bf16[256,2,192]{0,2,1:T(8,128)(2,1)} %fusion.218), channel_id=1, source_target_pairs={{0,4},{4,8},{8,12},{12,16},{16,20},{20,24},{24,28},{28,0},{1,5},{5... | collective-permute-start | bytes 589832 | tf_op jit(solution)/shard_map/while/body/eval_jaxpr/ppermute | solution.py:14
  574.0 23.9 %collective-permute-start.6 = (bf16[256,2,192]{0,2,1:T(8,128)(2,1)}, bf16[256,2,192]{0,2,1:T(8,128)(2,1)}, u32[]{:S(2)}, u32[]{:S(2)}) collective-permute-start(bf16[256,2,192]{0,2,1:T(8,128)(2,1)} %fusion.222), channel_id=1, source_target_pairs={{0,4},{4,8},{8,12},{12,16},{16,20},{20,24},{24,28},{28,0},{1,5},{5... | collective-permute-start | bytes 589832 | tf_op jit(solution)/shard_map/while/body/eval_jaxpr/ppermute | solution.py:14
  621.6 32.3 %collective-permute-start = (bf16[256,2,192]{0,2,1:T(8,128)(2,1)S(1)}, bf16[256,2,192]{0,2,1:T(8,128)(2,1)}, u32[]{:S(2)}, u32[]{:S(2)}) collective-permute-start(bf16[256,2,192]{0,2,1:T(8,128)(2,1)S(1)} %get-tuple-element.1792), channel_id=1, source_target_pairs={{0,4},{4,8},{8,12},{12,16},{16,20},{20,24},{24,28},{28,0},{1,5},{5... | collective-permute-start | bytes 589832 | tf_op jit(solution)/shard_map/while/body/eval_jaxpr/ppermute | solution.py:14
  621.6 33.7 %collective-permute-start.2 = (bf16[256,2,192]{0,2,1:T(8,128)(2,1)}, bf16[256,2,192]{0,2,1:T(8,128)(2,1)}, u32[]{:S(2)}, u32[]{:S(2)}) collective-permute-start(bf16[256,2,192]{0,2,1:T(8,128)(2,1)} %get-tuple-element.1793), channel_id=1, source_target_pairs={{0,4},{4,8},{8,12},{12,16},{16,20},{20,24},{24,28},{28,0},{1,5},{5... | collective-permute-start | bytes 589832 | tf_op jit(solution)/shard_map/while/body/eval_jaxpr/ppermute | solution.py:14
  634.1 22.8 %collective-permute-start.4 = (bf16[256,2,192]{0,2,1:T(8,128)(2,1)}, bf16[256,2,192]{0,2,1:T(8,128)(2,1)}, u32[]{:S(2)}, u32[]{:S(2)}) collective-permute-start(bf16[256,2,192]{0,2,1:T(8,128)(2,1)} %fusion.218), channel_id=1, source_target_pairs={{0,4},{4,8},{8,12},{12,16},{16,20},{20,24},{24,28},{28,0},{1,5},{5... | collective-permute-start | bytes 589832 | tf_op jit(solution)/shard_map/while/body/eval_jaxpr/ppermute | solution.py:14
  635.9 23.9 %collective-permute-start.6 = (bf16[256,2,192]{0,2,1:T(8,128)(2,1)}, bf16[256,2,192]{0,2,1:T(8,128)(2,1)}, u32[]{:S(2)}, u32[]{:S(2)}) collective-permute-start(bf16[256,2,192]{0,2,1:T(8,128)(2,1)} %fusion.222), channel_id=1, source_target_pairs={{0,4},{4,8},{8,12},{12,16},{16,20},{20,24},{24,28},{28,0},{1,5},{5... | collective-permute-start | bytes 589832 | tf_op jit(solution)/shard_map/while/body/eval_jaxpr/ppermute | solution.py:14
  683.3 34.1 %collective-permute-start = (bf16[256,2,192]{0,2,1:T(8,128)(2,1)S(1)}, bf16[256,2,192]{0,2,1:T(8,128)(2,1)}, u32[]{:S(2)}, u32[]{:S(2)}) collective-permute-start(bf16[256,2,192]{0,2,1:T(8,128)(2,1)S(1)} %get-tuple-element.1792), channel_id=1, source_target_pairs={{0,4},{4,8},{8,12},{12,16},{16,20},{20,24},{24,28},{28,0},{1,5},{5... | collective-permute-start | bytes 589832 | tf_op jit(solution)/shard_map/while/body/eval_jaxpr/ppermute | solution.py:14
  684.9 33.9 %collective-permute-start.2 = (bf16[256,2,192]{0,2,1:T(8,128)(2,1)}, bf16[256,2,192]{0,2,1:T(8,128)(2,1)}, u32[]{:S(2)}, u32[]{:S(2)}) collective-permute-start(bf16[256,2,192]{0,2,1:T(8,128)(2,1)} %get-tuple-element.1793), channel_id=1, source_target_pairs={{0,4},{4,8},{8,12},{12,16},{16,20},{20,24},{24,28},{28,0},{1,5},{5... | collective-permute-start | bytes 589832 | tf_op jit(solution)/shard_map/while/body/eval_jaxpr/ppermute | solution.py:14
  750.1 33.9 %collective-permute-start = (bf16[256,2,192]{0,2,1:T(8,128)(2,1)S(1)}, bf16[256,2,192]{0,2,1:T(8,128)(2,1)}, u32[]{:S(2)}, u32[]{:S(2)}) collective-permute-start(bf16[256,2,192]{0,2,1:T(8,128)(2,1)S(1)} %get-tuple-element.1792), channel_id=1, source_target_pairs={{0,4},{4,8},{8,12},{12,16},{16,20},{20,24},{24,28},{28,0},{1,5},{5... | collective-permute-start | bytes 589832 | tf_op jit(solution)/shard_map/while/body/eval_jaxpr/ppermute | solution.py:14
  750.1 35.3 %collective-permute-start.2 = (bf16[256,2,192]{0,2,1:T(8,128)(2,1)}, bf16[256,2,192]{0,2,1:T(8,128)(2,1)}, u32[]{:S(2)}, u32[]{:S(2)}) collective-permute-start(bf16[256,2,192]{0,2,1:T(8,128)(2,1)} %get-tuple-element.1793), channel_id=1, source_target_pairs={{0,4},{4,8},{8,12},{12,16},{16,20},{20,24},{24,28},{28,0},{1,5},{5... | collective-permute-start | bytes 589832 | tf_op jit(solution)/shard_map/while/body/eval_jaxpr/ppermute | solution.py:14
  763.1 24.1 %collective-permute-start.4 = (bf16[256,2,192]{0,2,1:T(8,128)(2,1)}, bf16[256,2,192]{0,2,1:T(8,128)(2,1)}, u32[]{:S(2)}, u32[]{:S(2)}) collective-permute-start(bf16[256,2,192]{0,2,1:T(8,128)(2,1)} %fusion.218), channel_id=1, source_target_pairs={{0,4},{4,8},{8,12},{12,16},{16,20},{20,24},{24,28},{28,0},{1,5},{5... | collective-permute-start | bytes 589832 | tf_op jit(solution)/shard_map/while/body/eval_jaxpr/ppermute | solution.py:14
  764.8 24.4 %collective-permute-start.6 = (bf16[256,2,192]{0,2,1:T(8,128)(2,1)}, bf16[256,2,192]{0,2,1:T(8,128)(2,1)}, u32[]{:S(2)}, u32[]{:S(2)}) collective-permute-start(bf16[256,2,192]{0,2,1:T(8,128)(2,1)} %fusion.222), channel_id=1, source_target_pairs={{0,4},{4,8},{8,12},{12,16},{16,20},{20,24},{24,28},{28,0},{1,5},{5... | collective-permute-start | bytes 589832 | tf_op jit(solution)/shard_map/while/body/eval_jaxpr/ppermute | solution.py:14
  821.0 119.5 %all-reduce.18.cloned.1.call-start = ((), (), s32[]{:S(2)}) async-start(), calls=%async_computation.8 | async-start | bytes 2359296 | tf_op jit(solution)/shard_map/psum | solution.py:393
  (128 other events, 1609.8 us)
Sparse Core Ops, SparseCore 0:
  17.8 47.9 all-gather.4
  67.8 43.4 all-gather.2
  227.9 32.7 all-reduce.13
  463.6 67.2 all-reduce.19
  821.2 33.6 all-reduce.15
  859.1 81.3 all-reduce.17
where the time goes:
time: 966 us; the launch traced here: 953 us
  waiting for transfers between devices  316 us (33%)
  local copies, waits for them, and re-layouts  279 us (29%)
  matrix products  130 us (13%)
  other arithmetic  112 us (12%)
  starting transfers between devices  61.1 us (6%)
  blocking collectives  37.5 us (4%)
  between operations  15.4 us (2%)
    reshape x16, local copies, waits for them, and re-layouts, offset_bias(): skewed = tiled.reshape(head_count, query_len, line_len)  62.6 us
    all_to_all x2, waiting for transfers between devices, send_slots(): lax.all_to_all(packed.reshape(expert_count, capacity, model_width), 'ctx'...  61.9 us
    psum x1, waiting for transfers between devices, unit_return(): lax.psum(returned.astype(jnp.bfloat16), 'wa').astype(jnp.float32)  57.5 us
    all_to_all x2, waiting for transfers between devices, unit_return(): lax.all_to_all(partial_rows.astype(jnp.bfloat16), 'ctx', split_axis=1, co...  46 us
    slice x24, local copies, waits for them, and re-layouts, offset_bias(): return skewed[:, :, query_len - 1:query_len - 1 + key_len]  44.5 us
    ppermute x32, starting transfers between devices, passed_along(): return lax.ppermute(value, axis, pairs)  43.5 us
    all_gather x1, waiting for transfers between devices, body(): lax.all_gather(key_rows, 'ctx', axis=0, tiled=True)  42.2 us
    while x124, local copies, waits for them, and re-layouts  37.8 us
  transfers between devices with their start and end apart: 42, of which 16 were waited for; matrix products, arithmetic and copies ran while one was open for 36% of the time, Pallas kernels for 0%

commit v1 on v0

v1 whole, which is shorter than its diff:
```python
import functools

import jax
import jax.numpy as jnp
from jax import lax
from jax.experimental import pallas as pl
from jax.experimental.pallas import tpu as pltpu
from jax.sharding import PartitionSpec as P

eps = 1e-06
highest = lax.Precision.HIGHEST


def gelu_tanh(values):
    return jax.nn.gelu(values, approximate=True)


def rms_forward(flat_rows, gain):
    scale = lax.rsqrt(jnp.mean(flat_rows * flat_rows, axis=-1, keepdims=True) + eps)
    return (flat_rows * scale * gain, scale)


def rms_backward(flat_rows, scale, gain, grad_out):
    weighted = grad_out * gain
    inner_mean = jnp.mean(weighted * flat_rows, axis=-1, keepdims=True)
    grad_rows = scale * weighted - flat_rows * scale * scale * scale * inner_mean
    grad_gain = jnp.sum(grad_out * flat_rows * scale, axis=0)
    return (grad_rows, grad_gain)


def spread_bias(base, wide_ref):
    rows = base.shape[0]
    wide_ref[0:rows, :] = base
    while rows < wide_ref.shape[0]:
        wide_ref[rows : 2 * rows, :] = pltpu.roll(wide_ref[0:rows, :], rows, 1)
        rows = 2 * rows


def fold_diagonals(wide_ref):
    rows, width = wide_ref.shape
    while rows > 8:
        rows = rows // 2
        moved = pltpu.roll(wide_ref[rows : 2 * rows, :], width - rows, 1)
        wide_ref[0:rows, :] = wide_ref[0:rows, :] + moved
    return wide_ref[0:8, :]


def over_blocks(count, init, step):
    group = 8 if count % 8 == 0 else 1

    def some(turn, state):
        for inner in range(group):
            state = step(turn * group + inner, state)
        return state

    if count == group:
        return some(0, init)
    return lax.fori_loop(0, count // group, some, init)


def nt_dot(left, right):
    return lax.dot_general(left, right, (((1,), (1,)), ((), ())), preferred_element_type=jnp.float32)


def lanes(number, width):
    start = number * width
    return pl.ds(start if isinstance(start, int) else pl.multiple_of(start, width), width)


def attend_kernel(head_dim, base_ref, query_ref, kv_ref, out_ref, lse_ref, wide_ref, score_ref):
    heads = base_ref.shape[0]
    blocks, head_rows, tokens = kv_ref.shape
    block = wide_ref.shape[0]
    seqs = tokens // block
    for head in range(heads):
        spread_bias(base_ref[head], wide_ref)
        key_at = slice(head * head_dim, (head + 1) * head_dim)
        value_at = slice(head_rows // 2 + head * head_dim, head_rows // 2 + (head + 1) * head_dim)
        for seq in range(seqs):
            here = slice(seq * block, (seq + 1) * block)
            query = query_ref[here, key_at]

            def score_step(number, top):
                scores = jnp.dot(query, kv_ref[number, key_at, here], preferred_element_type=jnp.float32)
                scores = scores + wide_ref[:, lanes(number, block)]
                score_ref[number] = scores
                return jnp.maximum(top, scores)

            top = over_blocks(blocks, jnp.full((block, block), -3e38, jnp.float32), score_step)
            top = jnp.max(top, axis=1, keepdims=True)

            def value_step(number, state):
                mass, total = state
                weights = jnp.exp(score_ref[number] - top)
                total = total + nt_dot(weights.astype(jnp.bfloat16), kv_ref[number, value_at, here])
                return (mass + weights, total)

            mass, total = over_blocks(
                blocks,
                (jnp.zeros((block, block), jnp.float32), jnp.zeros((block, head_dim), jnp.float32)),
                value_step,
            )
            mass = jnp.sum(mass, axis=1, keepdims=True)
            out_ref[here, key_at] = total / mass
            lse_ref[head, here, :] = top + jnp.log(mass)


def attend_back_kernel(
    head_dim,
    base_ref,
    query_ref,
    query_t_ref,
    grad_ref,
    grad_t_ref,
    out_ref,
    lse_ref,
    kv_ref,
    dquery_ref,
    dkv_ref,
    dline_ref,
    wide_ref,
    fold_ref,
):
    heads = base_ref.shape[0]
    blocks, head_rows, tokens = kv_ref.shape
    block = wide_ref.shape[0]
    seqs = tokens // block
    for head in range(heads):
        spread_bias(base_ref[head], wide_ref)
        key_at = slice(head * head_dim, (head + 1) * head_dim)
        value_at = slice(head_rows // 2 + head * head_dim, head_rows // 2 + (head + 1) * head_dim)
        deltas = [
            jnp.sum(
                grad_ref[seq * block : (seq + 1) * block, key_at].astype(jnp.float32)
                * out_ref[seq * block : (seq + 1) * block, key_at],
                axis=1,
                keepdims=True,
            )
            for seq in range(seqs)
        ]

        def step(number, state):
            bias = wide_ref[:, lanes(number, block)]
            new_state, seen = [], None
            for seq in range(seqs):
                here = slice(seq * block, (seq + 1) * block)
                key_t = kv_ref[number, key_at, here]
                scores = jnp.dot(query_ref[here, key_at], key_t, preferred_element_type=jnp.float32)
                weights = jnp.exp(scores + bias - lse_ref[head, here, :])
                grad_weights = jnp.dot(
                    grad_ref[here, key_at],
                    kv_ref[number, value_at, here],
                    preferred_element_type=jnp.float32,
                )
                grad_scores = (weights * (grad_weights - deltas[seq])).astype(jnp.bfloat16)
                dkv_ref[number, key_at, here] = jnp.dot(
                    query_t_ref[key_at, here], grad_scores, preferred_element_type=jnp.float32
                ).astype(jnp.bfloat16)
                dkv_ref[number, value_at, here] = jnp.dot(
                    grad_t_ref[key_at, here],
                    weights.astype(jnp.bfloat16),
                    preferred_element_type=jnp.float32,
                ).astype(jnp.bfloat16)
                new_state.append(state[seq] + nt_dot(grad_scores, key_t))
                wide = grad_scores.astype(jnp.float32)
                seen = wide if seen is None else seen + wide
            fold_ref[:, lanes(number, block)] = seen
            return tuple(new_state)

        totals = over_blocks(
            blocks, tuple(jnp.zeros((block, head_dim), jnp.float32) for _ in range(seqs)), step
        )
        for seq in range(seqs):
            dquery_ref[seq * block : (seq + 1) * block, key_at] = totals[seq]
        fold_ref[:, blocks * block :] = jnp.zeros((block, block), jnp.float32)
        dline_ref[head] = fold_diagonals(fold_ref)


def in_vmem(count):
    return [pl.BlockSpec(memory_space=pltpu.VMEM)] * count


params = pltpu.CompilerParams(vmem_limit_bytes=58 * 1024 * 1024)


def attend(base, query, kv_all, head_dim):
    heads, _, width = base.shape
    blocks, _, tokens = kv_all.shape
    block = width // (blocks + 1)
    return pl.pallas_call(
        functools.partial(attend_kernel, head_dim),
        out_shape=(
            jax.ShapeDtypeStruct(query.shape, jnp.float32),
            jax.ShapeDtypeStruct((heads, tokens, 1), jnp.float32),
        ),
        in_specs=in_vmem(3),
        out_specs=tuple(in_vmem(2)),
        scratch_shapes=[
            pltpu.VMEM((block, width), jnp.float32),
            pltpu.VMEM((blocks, block, block), jnp.float32),
        ],
        compiler_params=params,
    )(base, query, kv_all)


def attend_back(base, query, query_t, grad, grad_t, attended, lse, kv_all, head_dim):
    heads, _, width = base.shape
    blocks = kv_all.shape[0]
    block = width // (blocks + 1)
    return pl.pallas_call(
        functools.partial(attend_back_kernel, head_dim),
        out_shape=(
            jax.ShapeDtypeStruct(query.shape, jnp.float32),
            jax.ShapeDtypeStruct(kv_all.shape, jnp.bfloat16),
            jax.ShapeDtypeStruct(base.shape, jnp.float32),
        ),
        in_specs=in_vmem(8),
        out_specs=tuple(in_vmem(3)),
        scratch_shapes=[
            pltpu.VMEM((block, width), jnp.float32),
            pltpu.VMEM((block, width), jnp.float32),
        ],
        compiler_params=params,
    )(base, query, query_t, grad, grad_t, attended, lse, kv_all)


def f32_dot(spec, left, right):
    return jnp.einsum(spec, left, right, preferred_element_type=jnp.float32)


def low(values):
    return values.astype(jnp.bfloat16)


def body(
    inputs,
    upstream,
    gain_attn,
    w_query,
    w_key,
    w_value,
    w_proj,
    rel_bias,
    gain_ffn,
    w_router,
    w_expin,
    w_expout,
    routes,
    bucket_table,
):
    block_len, seq_count, model_width = inputs.shape
    ctx_size = lax.axis_size("ctx")
    wa_size = lax.axis_size("wa")
    seq_len = block_len * ctx_size
    tok_count = block_len * seq_count
    head_local = rel_bias.shape[1]
    head_cols = w_query.shape[1]
    head_dim = head_cols // head_local
    bucket_count = rel_bias.shape[0]
    expert_count = w_router.shape[1]
    capacity = 2 * tok_count // expert_count
    my_index = lax.axis_index("ctx")
    wa_index = lax.axis_index("wa")

    def by_sequence(rows):
        return jnp.transpose(rows, (1, 0, 2)).reshape(tok_count, rows.shape[2])

    def by_position(rows):
        return jnp.transpose(rows.reshape(seq_count, block_len, model_width), (1, 0, 2))

    flat_rows = by_sequence(inputs)
    grad_rows = by_sequence(upstream)
    normed1, scale1 = rms_forward(flat_rows, gain_attn)
    normed1_low = low(normed1)
    w_kv = jnp.concatenate([w_key, w_value], axis=1)
    kv_t = low(f32_dot("ck,tc->kt", w_kv, normed1_low))
    kv_all = lax.all_gather(kv_t, "ctx", axis=0)
    query_low = low(f32_dot("tc,ck->tk", normed1_low, w_query))
    query_t = query_low.T

    width = seq_len + block_len
    window = lax.dynamic_slice_in_dim(
        jnp.pad(bucket_table, (0, 1)), seq_len - block_len - my_index * block_len, width
    )
    bucket_ids = jnp.arange(bucket_count, dtype=jnp.int32)
    in_bucket = (window[None, :] == bucket_ids[:, None]).astype(jnp.float32)
    line = jnp.einsum("bh,bj->hj", rel_bias, in_bucket, precision=highest)
    base = jnp.stack([jnp.roll(line, row - (block_len - 1), axis=1) for row in range(8)], axis=1)

    route_flat = by_sequence(routes).reshape(tok_count)
    expert_ids = jnp.arange(expert_count, dtype=jnp.int32)
    chosen = route_flat[:, None] == expert_ids[None, :]
    chosen_float = chosen.astype(jnp.float32)
    token_ids = jnp.arange(tok_count, dtype=jnp.int32)
    earlier = low(token_ids[:, None] > token_ids[None, :])
    ranks = f32_dot("tu,ue->te", earlier, low(chosen_float))
    slot_rank = jnp.sum(ranks * chosen_float, axis=1).astype(jnp.int32)
    part_cap = capacity // wa_size
    part_rows = expert_count * part_cap
    slot_index = (slot_rank // part_cap) * part_rows + route_flat * part_cap + slot_rank % part_cap
    own_slots = wa_index * part_rows + jnp.arange(part_rows, dtype=jnp.int32)
    dispatch = low(own_slots[:, None] == slot_index[None, :])
    all_slots = jnp.arange(wa_size * part_rows, dtype=jnp.int32)
    combine = low(slot_index[:, None] == all_slots[None, :])

    attended, lse = attend(base, query_low, kv_all, head_dim)
    attended_low = low(attended)
    attn_share = f32_dot("tk,kd->td", attended_low, w_proj)
    attn_out = lax.psum(low(attn_share), "wa").astype(jnp.float32)
    hidden1 = flat_rows + attn_out
    normed2, scale2 = rms_forward(hidden1, gain_ffn)
    normed2_low = low(normed2)
    logits = f32_dot("td,de->te", normed2_low, w_router)
    router_prob = jax.nn.softmax(logits, axis=-1)
    gate_value = jnp.sum(router_prob * chosen_float, axis=1)
    grad_expert = low(gate_value[:, None] * grad_rows)

    both = jnp.concatenate([normed2_low, grad_expert], axis=1)
    packed = low(f32_dot("st,td->sd", dispatch, both))
    landed = lax.all_to_all(packed, "ctx", split_axis=0, concat_axis=0, tiled=True)
    rows_in = lax.all_gather(landed, "wa", axis=0, tiled=True)
    received = rows_in[:, :model_width]
    grad_received = rows_in[:, model_width:]
    w_in, w_out = w_expin[0], w_expout[0]
    pre_act = f32_dot("rd,df->rf", received, w_in)
    activated, gelu_back = jax.vjp(gelu_tanh, pre_act)
    activated_low = low(activated)
    expert_part = f32_dot("rf,fd->rd", activated_low, w_out)
    grad_act = f32_dot("rd,fd->rf", grad_received, w_out)
    grad_pre = low(gelu_back(grad_act)[0])
    grad_inpart = f32_dot("rf,df->rd", grad_pre, w_in)
    rows_out = jnp.concatenate([low(expert_part), low(grad_inpart)], axis=1)
    summed_part = lax.psum_scatter(rows_out, "wa", scatter_dimension=0, tiled=True)
    returned = lax.all_to_all(summed_part, "ctx", split_axis=0, concat_axis=0, tiled=True)
    slot_rows = lax.all_gather(returned, "wa", axis=0, tiled=True)
    grad_wout = f32_dot("rf,rd->fd", activated_low, grad_received)[None]
    grad_win = f32_dot("rd,rf->df", received, grad_pre)[None]
    token_rows = f32_dot("ts,sd->td", combine, slot_rows)
    expert_out = token_rows[:, :model_width]
    grad_from_experts = token_rows[:, model_width:]

    output_rows = hidden1 + gate_value[:, None] * expert_out
    grad_gate = jnp.sum(grad_rows * expert_out, axis=1)
    grad_logits = router_prob * (chosen_float - gate_value[:, None]) * grad_gate[:, None]
    router_float = w_router.astype(jnp.float32)
    grad_normed2 = grad_from_experts + jnp.einsum(
        "te,de->td", grad_logits, router_float, precision=highest
    )
    grad_router = jnp.einsum(
        "td,te->de", normed2_low.astype(jnp.float32), grad_logits, precision=highest
    )
    grad_norm2_in, grad_gain2 = rms_backward(hidden1, scale2, gain_ffn, grad_normed2)
    grad_hidden1 = grad_rows + grad_norm2_in
    grad_attn_low = low(grad_hidden1)
    grad_proj = f32_dot("tk,td->kd", attended_low, grad_attn_low)
    grad_attended = low(f32_dot("td,kd->tk", grad_attn_low, w_proj))
    dquery, dkv, dline = attend_back(
        base,
        query_low,
        query_t,
        grad_attended,
        grad_attended.T,
        attended,
        lse,
        kv_all,
        head_dim,
    )
    dkv_t = lax.psum_scatter(dkv, "ctx", scatter_dimension=0)
    folded = sum(jnp.roll(dline[:, row, :], block_len - 1 - row, axis=1) for row in range(8))
    grad_bias = jnp.einsum("bj,hj->bh", in_bucket, folded, precision=highest)
    dquery_low = low(dquery)
    grad_wq = f32_dot("tc,tk->ck", normed1_low, dquery_low)
    grad_wkv = f32_dot("tc,kt->ck", normed1_low, dkv_t)
    grad_normed1_part = f32_dot("tk,ck->tc", dquery_low, w_query) + f32_dot(
        "kt,ck->tc", dkv_t, w_kv
    )
    grad_normed1 = lax.psum(low(grad_normed1_part), "wa").astype(jnp.float32)
    grad_norm1_in, grad_gain1 = rms_backward(flat_rows, scale1, gain_attn, grad_normed1)
    grad_inputs = grad_hidden1 + grad_norm1_in

    def over_ctx(values):
        return lax.psum(low(values), "ctx").astype(jnp.float32)

    sum_proj = over_ctx(grad_proj)
    sum_router = over_ctx(grad_router)
    sum_gain2 = over_ctx(grad_gain2)
    sum_wq = over_ctx(grad_wq)
    sum_bias = over_ctx(grad_bias)
    sum_wkv = over_ctx(grad_wkv)
    sum_gain1 = over_ctx(grad_gain1)
    return (
        by_position(output_rows),
        by_position(grad_inputs),
        sum_gain1,
        sum_wq,
        sum_wkv[:, :head_cols],
        sum_wkv[:, head_cols:],
        sum_proj,
        sum_bias,
        sum_gain2,
        sum_router,
        grad_win,
        grad_wout,
    )


def solution(mesh):
    in_specs = (
        P("ctx", None, None),
        P("ctx", None, None),
        P(),
        P(None, "wa"),
        P(None, "wa"),
        P(None, "wa"),
        P("wa", None),
        P(None, "wa"),
        P(),
        P(),
        P("ctx", None, "wa"),
        P("ctx", "wa", None),
        P("ctx", None, None),
        P(),
    )
    out_specs = (
        P("ctx", None, None),
        P("ctx", None, None),
        P(),
        P(None, "wa"),
        P(None, "wa"),
        P(None, "wa"),
        P("wa", None),
        P(None, "wa"),
        P(),
        P(),
        P("ctx", None, "wa"),
        P("ctx", "wa", None),
    )
    return jax.shard_map(body, mesh=mesh, in_specs=in_specs, out_specs=out_specs, check_vma=False)
```

time: 966 us -> 533 us (0.55)
  local copies, waits for them, and re-layouts: 279 us -> 40.2 us
  matrix products: 130 us -> 40.7 us
  other arithmetic: 112 us -> 30.6 us
  starting transfers between devices: 61.1 us -> 0.89 us
  blocking collectives: 37.5 us -> 88 us
  waiting for transfers between devices: 316 us -> 281 us
  Pallas kernels: 0 us -> 27.5 us
    all_to_all x4 -> x0, waiting for transfers between devices: 108 us -> none  [the longest x2 61.9 us: send_slots(): lax.all_to_all(packed.reshape(expert_count, capacity, model_width), 'ctx'...]
    reduce_scatter x0 -> x2, waiting for transfers between devices: none -> 98.5 us  [the longest x1 60.5 us: body(): dkv_t = lax.psum_scatter(dkv, 'ctx', scatter_dimension=0)]
    reshape x34 -> x2, local copies, waits for them, and re-layouts: 98.4 us -> 6.18 us  [by_position(): rows.reshape(seq_count, block_len, model_width)]
    dot_general x93 -> x21, matrix products: 128 us -> 38.5 us  [the longest x19 37.3 us: f32_dot(): return jnp.einsum(spec, left, right, preferred_element_type=jnp.float32)]
    slice x48 -> x34, local copies, waits for them, and re-layouts: 65.6 us -> 9.76 us  [the longest x16 7.97 us: body(): jnp.roll(line, row - (block_len - 1), axis=1)]
    psum x4 -> x3, waiting for transfers between devices: 147 us -> 92.3 us  [the longest x1 39.7 us: over_ctx(): return lax.psum(low(values), 'ctx').astype(jnp.float32)]
    all_to_all x0 -> x2, blocking collectives: none -> 50.3 us  [the longest x1 25.6 us: body(): lax.all_to_all(summed_part, 'ctx', split_axis=0, concat_axis=0, tiled=True)]
    all_gather x2 -> x3, waiting for transfers between devices: 42.2 us -> 90.3 us  [the longest x1 36.8 us: body(): kv_all = lax.all_gather(kv_t, 'ctx', axis=0)]
  transfers between devices with their start and end apart: 42 -> 8, of which waited for: 16 -> 8; matrix products, arithmetic and copies ran while one was open for 36% -> 12% of each run, Pallas kernels for 0% -> 0%
where the time goes in v1:
time: 533 us; the launch traced here: 524 us
  waiting for transfers between devices  281 us (53%)
  blocking collectives  88 us (17%)
  matrix products  40.7 us (8%)
  local copies, waits for them, and re-layouts  40.2 us (8%)
  other arithmetic  30.6 us (6%)
  Pallas kernels  27.5 us (5%)
  between operations  15.2 us (3%)
    reduce_scatter x1, waiting for transfers between devices, body(): dkv_t = lax.psum_scatter(dkv, 'ctx', scatter_dimension=0)  60.5 us
    psum x1, waiting for transfers between devices, over_ctx(): return lax.psum(low(values), 'ctx').astype(jnp.float32)  39.7 us
    reduce_scatter x1, waiting for transfers between devices, body(): lax.psum_scatter(rows_out, 'wa', scatter_dimension=0, tiled=True)  38.1 us
    psum x1, blocking collectives, over_ctx(): return lax.psum(low(values), 'ctx').astype(jnp.float32)  37.7 us
    dot_general x19, matrix products, f32_dot(): return jnp.einsum(spec, left, right, preferred_element_type=jnp.float32)  37.3 us
    all_gather x1, waiting for transfers between devices, body(): kv_all = lax.all_gather(kv_t, 'ctx', axis=0)  36.8 us
    psum x1, waiting for transfers between devices, body(): attn_out = lax.psum(low(attn_share), 'wa').astype(jnp.float32)  29.2 us
    all_gather x1, waiting for transfers between devices, body(): rows_in = lax.all_gather(landed, 'wa', axis=0, tiled=True)  26.8 us
  transfers between devices with their start and end apart: 8, of which 8 were waited for; matrix products, arithmetic and copies ran while one was open for 12% of the time, Pallas kernels for 0%

profile of v1, /device:TPU:0, one launch (start us, length us, event | category | flops | bytes accessed | tf_op | source)
XLA Modules:
  0.0 524.4 jit_solution(10458654728079456620)
XLA Ops:
  38.9 36.8 %all-gather.9.cloned.1.call-done = bf16[3072,512]{1,0:T(8,128)(2,1)} async-done(((bf16[384,512]{1,0:T(8,128)(2,1)}), bf16[3072,512]{1,0:T(8,128)(2,1)}) %all-gather.9.cloned.1.call-update) | async-done | bytes 3145744 | tf_op jit(solution)/shard_map/all_gather | solution.py:277
  75.7 8.2 %shard_map.229 = (f32[512,192]{1,0:T(8,128)}, f32[3,512,1]{2,1,0:T(8,128)}) custom-call(f32[3,8,2304]{2,1,0:T(8,128)} %stack.35.base_ref, bf16[512,192]{1,0:T(8,128)(2,1)} %copy.57.query_ref, bf16[8,384,512]{2,1,0:T(8,128)(2,1)} %bitcast.121), custom_call_target="tpu_custom_call" | custom-call | tf_op jit(solution)/shard_map/pallas_call | solution.py:190
  86.9 2.7 copy.58
  90.4 29.2 %all-reduce.7.cloned.1.call-done = bf16[512,768]{1,0:T(8,128)(2,1)} async-done(((bf16[512,768]{1,0:T(8,128)(2,1)}), bf16[512,768]{1,0:T(8,128)(2,1)}) %all-reduce.7.cloned.1.call-update) | async-done | bytes 786448 | tf_op jit(solution)/shard_map/psum | solution.py:309
  124.3 24.7 %all_to_all.24 = bf16[8,32,1536]{2,1,0:T(8,128)(2,1)} all-to-all(bf16[8,32,1536]{2,1,0:T(8,128)(2,1)S(1)} %bitcast.134), channel_id=1, replica_groups=mesh['ctx'=8,'wa'=4] {'ctx'}, dimensions={0} | all-to-all | bytes 1572864 | tf_op jit(solution)/shard_map/all_to_all | solution.py:320
  149.5 26.8 %all-gather.5.cloned.1.call-done = bf16[1024,1536]{1,0:T(8,128)(2,1)} async-done(((bf16[256,1536]{1,0:T(8,128)(2,1)}), bf16[1024,1536]{1,0:T(8,128)(2,1)}) %all-gather.5.cloned.1.call-update) | async-done | bytes 3145744 | tf_op jit(solution)/shard_map/all_gather | solution.py:321
  176.3 3.1 fusion.29
  182.5 3.0 fusion.6
  190.2 38.1 %reduce-scatter.3.cloned.1.call-done = bf16[256,1536]{0,1:T(8,128)(2,1)} async-done(((bf16[1024,1536]{0,1:T(8,128)(2,1)}), bf16[256,1536]{0,1:T(8,128)(2,1)}) %reduce-scatter.3.cloned.1.call-update) | async-done | bytes 786448 | tf_op jit(solution)/shard_map/reduce_scatter | solution.py:333
  229.7 25.6 %all_to_all.25 = bf16[8,32,1536]{2,1,0:T(8,128)(2,1)} all-to-all(bf16[8,32,1536]{2,1,0:T(8,128)(2,1)S(1)} %bitcast.128), channel_id=1, replica_groups=mesh['ctx'=8,'wa'=4] {'ctx'}, dimensions={0} | all-to-all | bytes 1572864 | tf_op jit(solution)/shard_map/all_to_all | solution.py:334
  255.4 26.7 %all-gather.7.cloned.1.call-done = bf16[1024,1536]{1,0:T(8,128)(2,1)} async-done(((bf16[256,1536]{1,0:T(8,128)(2,1)}), bf16[1024,1536]{1,0:T(8,128)(2,1)}) %all-gather.7.cloned.1.call-update) | async-done | bytes 3145744 | tf_op jit(solution)/shard_map/all_gather | solution.py:335
  282.1 3.7 fusion.7
  285.9 3.5 fusion.19
  294.1 19.3 %shard_map.230 = (f32[512,192]{1,0:T(8,128)}, bf16[8,384,512]{2,1,0:T(8,128)(2,1)}, f32[3,8,2304]{2,1,0:T(8,128)}) custom-call(f32[3,8,2304]{2,1,0:T(8,128)} %stack.35.base_ref, bf16[512,192]{1,0:T(8,128)(2,1)} %copy.57.query_ref, bf16[192,512]{1,0:T(8,128)(2,1)} %bitcast.129, bf16[512,192]{1,0:T(8,128)(2,1)} %copy.62.grad_ref, bf16[192,512]{1,0:T(8,128)(2,1)} %bitcast.130, ...), custom_call_target="tpu_custom_call" | custom-call | tf_op jit(solution)/shard_map/pallas_call | solution.py:210
  314.1 2.5 fusion.21
  316.6 4.4 convolution_bitcast_fusion.2
  321.1 3.2 convolution_bitcast_fusion.1
  327.7 60.5 %reduce-scatter.5.cloned.1.call-done = bf16[1,384,512]{2,1,0:T(8,128)(2,1)} async-done(((bf16[8,384,512]{2,1,0:T(8,128)(2,1)}), bf16[1,384,512]{2,1,0:T(8,128)(2,1)}) %reduce-scatter.5.cloned.1.call-update) | async-done | bytes 393232 | tf_op jit(solution)/shard_map/reduce_scatter | solution.py:368
  388.2 3.2 add_convert_fusion
  397.7 3.8 copy.81
  401.9 23.4 %all-reduce.9.cloned.1.call-done = bf16[512,768]{1,0:T(8,128)(2,1)} async-done(((bf16[512,768]{1,0:T(8,128)(2,1)}), bf16[512,768]{1,0:T(8,128)(2,1)}) %all-reduce.9.cloned.1.call-update) | async-done | bytes 786448 | tf_op jit(solution)/shard_map/psum | solution.py:377
  427.2 37.7 %all-reduce.1 = (bf16[768]{0:T(1024)(128)(2,1)S(1)}, bf16[32,3]{0,1:T(4,128)(2,1)S(1)}, bf16[768]{0:T(1024)(128)(2,1)S(1)}, bf16[768,8]{0,1:T(8,128)(2,1)S(1)}) all-reduce(bf16[768]{0:T(1024)(128)(2,1)S(1)} %get-tuple-element.48, bf16[32,3]{0,1:T(4,128)(2,1)S(1)} %convolution_convert_fusion.11, ...), channel_id=1, replica_groups=mesh['ctx'=8,'wa'=4] {'ctx'}, use_global_device_ids=true, to_apply=%region_14.15 | all-reduce | flops 7776 | bytes 31104 | tf_op jit(solution)/shard_map/psum | solution.py:382
  468.0 2.4 copy.80
  471.5 39.7 %all-reduce.11.cloned.1.call-done = (bf16[768,384]{1,0:T(8,128)(2,1)}, bf16[768,192]{0,1:T(8,128)(2,1)}, bf16[192,768]{1,0:T(8,128)(2,1)}) async-done(((bf16[768,384]{1,0:T(8,128)(2,1)}, bf16[768,192]{0,1:T(8,128)(2,1)}, bf16[192,768]{1,0:T(8,128)(2,1)}), (bf16[768,384]{1,0:T(8,128)(2,1)}, bf16[768,192]{0,1:T(8,128)(2,1)}, bf16[192,768]{1,0:T(8,128)(2,1)})) %all-reduce.11.cloned.1.call-update) | async-done | bytes 1179664 | tf_op jit(solution)/shard_map/psum | solution.py:382
  (266 shorter events, 76.9 us)
Async XLA Ops:
  7.2 172.2 %copy-start = (bf16[1,768,768]{2,1,0:T(8,128)(2,1)S(1)}, bf16[1,768,768]{2,1,0:T(8,128)(2,1)}, u32[]{:S(2)}) copy-start(bf16[1,768,768]{2,1,0:T(8,128)(2,1)} %param.25) | copy-start | bytes 3538948
  7.2 68.5 %all-gather.9.cloned.1.call-start = ((), (), s32[]{:S(2)}) async-start(), calls=%async_computation.10 | async-start | bytes 3538944 | tf_op jit(solution)/shard_map/all_gather | solution.py:277
  12.4 107.3 %all-reduce.7.cloned.1.call-start = ((), (), s32[]{:S(2)}) async-start(), calls=%async_computation.4 | async-start | bytes 1572864 | tf_op jit(solution)/shard_map/psum | solution.py:309
  75.7 8.2 %copy-start.20 = (bf16[192,768]{1,0:T(8,128)(2,1)S(1)}, bf16[192,768]{1,0:T(8,128)(2,1)}, u32[]{:S(2)}) copy-start(bf16[192,768]{1,0:T(8,128)(2,1)} %param.20) | copy-start | bytes 884740
  86.2 90.0 %all-gather.5.cloned.1.call-start = ((), (), s32[]{:S(2)}) async-start(), calls=%async_computation.5 | async-start | bytes 3932160 | tf_op jit(solution)/shard_map/all_gather | solution.py:321
  90.4 31.3 %copy-start.43 = (f32[768]{0:T(1024)S(1)}, f32[768]{0:T(1024)}, u32[]{:S(2)}) copy-start(f32[768]{0:T(1024)} %param.22) | copy-start | bytes 9220
  149.1 79.2 %reduce-scatter.3.cloned.1.call-start = ((), (), s32[]{:S(2)}) async-start(), calls=%async_computation.6 | async-start | bytes 3932160 | tf_op jit(solution)/shard_map/reduce_scatter | solution.py:333
  182.5 4.2 copy-start.67
  190.2 91.9 %all-gather.7.cloned.1.call-start = ((), (), s32[]{:S(2)}) async-start(), calls=%async_computation.7 | async-start | bytes 3932160 | tf_op jit(solution)/shard_map/all_gather | solution.py:335
  229.7 52.4 %copy-start.64 = (s32[512]{0:T(512)S(1)}, s32[512]{0:T(512)}, u32[]{:S(2)}) copy-start(s32[512]{0:T(512)} %fusion.73) | copy-start | bytes 6148
  255.3 30.5 %copy-start.39 = (f32[512]{0:T(512)S(1)}, f32[512]{0:T(512)}, u32[]{:S(2)}) copy-start(f32[512]{0:T(512)} %copy-done.38) | copy-start | bytes 6148
  255.3 132.9 %reduce-scatter.5.cloned.1.call-start = ((), (), s32[]{:S(2)}) async-start(), calls=%async_computation.8 | async-start | bytes 3538944 | tf_op jit(solution)/shard_map/reduce_scatter | solution.py:368
  313.5 111.9 %all-reduce.9.cloned.1.call-start = ((), (), s32[]{:S(2)}) async-start(), calls=%async_computation.9 | async-start | bytes 1572864 | tf_op jit(solution)/shard_map/psum | solution.py:377
  316.6 4.4 copy-start.66
  316.6 4.4 copy-start.70
  391.4 4.3 copy-start.13
  391.4 4.3 copy-start.17
  391.4 119.8 %all-reduce.11.cloned.1.call-start = ((), (), s32[]{:S(2)}) async-start(), calls=%async_computation.11 | async-start | bytes 2359296 | tf_op jit(solution)/shard_map/psum | solution.py:382
  397.5 3.9 copy-start.37
  397.6 3.9 copy-start.40
  397.6 27.7 %copy-start.34 = (f32[768]{0:T(1024)S(1)}, f32[768]{0:T(1024)}, u32[]{:S(2)}) copy-start(f32[768]{0:T(1024)} %param.16) | copy-start | bytes 9220
  397.6 27.7 %copy-start.55 = (f32[1,2,2,128]{3,1,2,0:T(2,128)S(1)}, f32[1,2,2,128]{3,1,2,0:T(2,128)}, u32[]{:S(2)}) copy-start(f32[1,2,2,128]{3,1,2,0:T(2,128)} %copy-done.54) | copy-start | bytes 6148
  401.5 25.6 %copy-start.61 = (bf16[768]{0:T(1024)(128)(2,1)S(1)}, bf16[768]{0:T(1024)(128)(2,1)}, u32[]{:S(2)}) copy-start(bf16[768]{0:T(1024)(128)(2,1)} %get-tuple-element.46) | copy-start | bytes 4612
  425.3 40.7 %copy-start.14 = (bf16[512,768]{1,0:T(8,128)(2,1)S(1)}, bf16[512,768]{1,0:T(8,128)(2,1)}, u32[]{:S(2)}) copy-start(bf16[512,768]{1,0:T(8,128)(2,1)} %all-reduce.9.cloned.1.call-done) | copy-start | bytes 2359300
  (57 other events, 130.9 us)
Sparse Core Ops, SparseCore 0:
  12.5 63.1 all-gather.8
  86.4 33.2 all-reduce.6
  149.2 27.0 all-gather.4
  190.3 37.9 reduce-scatter.2
  255.4 26.5 all-gather.6
  313.6 74.5 reduce-scatter.4
  391.6 33.7 all-reduce.8
  430.1 81.1 all-reduce.10

commit v2 on v1

--- a/solution.py
+++ b/solution.py
@@ -109,14 +109,11 @@
     head_dim,
     base_ref,
     query_ref,
-    query_t_ref,
     grad_ref,
-    grad_t_ref,
     out_ref,
     lse_ref,
     kv_ref,
     dquery_ref,
-    dkv_ref,
     dline_ref,
     wide_ref,
     fold_ref,
@@ -153,14 +150,6 @@
                     preferred_element_type=jnp.float32,
                 )
                 grad_scores = (weights * (grad_weights - deltas[seq])).astype(jnp.bfloat16)
-                dkv_ref[number, key_at, here] = jnp.dot(
-                    query_t_ref[key_at, here], grad_scores, preferred_element_type=jnp.float32
-                ).astype(jnp.bfloat16)
-                dkv_ref[number, value_at, here] = jnp.dot(
-                    grad_t_ref[key_at, here],
-                    weights.astype(jnp.bfloat16),
-                    preferred_element_type=jnp.float32,
-                ).astype(jnp.bfloat16)
                 new_state.append(state[seq] + nt_dot(grad_scores, key_t))
                 wide = grad_scores.astype(jnp.float32)
                 seen = wide if seen is None else seen + wide
@@ -174,6 +163,54 @@
             dquery_ref[seq * block : (seq + 1) * block, key_at] = totals[seq]
         fold_ref[:, blocks * block :] = jnp.zeros((block, block), jnp.float32)
         dline_ref[head] = fold_diagonals(fold_ref)
+
+
+def stat_row(ref, number, first, here, head, heads):
+    held = ref[number, first : first + 16, here].astype(jnp.float32)
+    return sum(held[part * heads + head : part * heads + head + 1, :] for part in range(3))
+
+
+def key_back_kernel(
+    head_dim, base_ref, key_ref, value_ref, query_ref, grad_ref, dkey_ref, dvalue_ref, wide_ref
+):
+    heads = base_ref.shape[0]
+    blocks, _, tokens = query_ref.shape
+    block = wide_ref.shape[0]
+    seqs = tokens // block
+    for head in range(heads):
+        spread_bias(base_ref[head], wide_ref)
+        head_at = slice(head * head_dim, (head + 1) * head_dim)
+
+        def step(number, state):
+            bias = wide_ref[:, lanes(number, block)]
+            new_state = []
+            for seq in range(seqs):
+                here = slice(seq * block, (seq + 1) * block)
+                query_t = query_ref[number, head_at, here]
+                grad_t = grad_ref[number, head_at, here]
+                lse = stat_row(query_ref, number, heads * head_dim, here, head, heads)
+                delta = stat_row(grad_ref, number, heads * head_dim, here, head, heads)
+                scores = jnp.dot(key_ref[here, head_at], query_t, preferred_element_type=jnp.float32)
+                weights = jnp.exp(scores + bias - lse)
+                grad_weights = jnp.dot(
+                    value_ref[here, head_at], grad_t, preferred_element_type=jnp.float32
+                )
+                grad_scores = (weights * (grad_weights - delta)).astype(jnp.bfloat16)
+                dkey, dvalue = state[seq]
+                new_state.append(
+                    (
+                        dkey + nt_dot(grad_scores, query_t),
+                        dvalue + nt_dot(weights.astype(jnp.bfloat16), grad_t),
+                    )
+                )
+            return tuple(new_state)
+
+        zero = jnp.zeros((block, head_dim), jnp.float32)
+        totals = over_blocks(blocks, tuple((zero, zero) for _ in range(seqs)), step)
+        for seq in range(seqs):
+            here = slice(seq * block, (seq + 1) * block)
+            dkey_ref[here, head_at] = totals[seq][0]
+            dvalue_ref[here, head_at] = totals[seq][1]
 
 
 def in_vmem(count):
@@ -203,7 +240,7 @@
     )(base, query, kv_all)
 
 
-def attend_back(base, query, query_t, grad, grad_t, attended, lse, kv_all, head_dim):
+def attend_back(base, query, grad, attended, lse, kv_all, head_dim):
     heads, _, width = base.shape
     blocks = kv_all.shape[0]
     block = width // (blocks + 1)
@@ -211,17 +248,43 @@
         functools.partial(attend_back_kernel, head_dim),
         out_shape=(
             jax.ShapeDtypeStruct(query.shape, jnp.float32),
-            jax.ShapeDtypeStruct(kv_all.shape, jnp.bfloat16),
             jax.ShapeDtypeStruct(base.shape, jnp.float32),
         ),
-        in_specs=in_vmem(8),
-        out_specs=tuple(in_vmem(3)),
+        in_specs=in_vmem(6),
+        out_specs=tuple(in_vmem(2)),
         scratch_shapes=[
             pltpu.VMEM((block, width), jnp.float32),
             pltpu.VMEM((block, width), jnp.float32),
         ],
         compiler_params=params,
-    )(base, query, query_t, grad, grad_t, attended, lse, kv_all)
+        cost_estimate=pl.CostEstimate(
+            flops=3 * 2 * query.size * (width - block), bytes_accessed=40_000_000, transcendentals=0
+        ),
+    )(base, query, grad, attended, lse, kv_all)
+
+
+def key_back(base, keys, values, query_all, grad_all, head_dim):
+    _, _, width = base.shape
+    block = width // (query_all.shape[0] + 1)
+    shape = jax.ShapeDtypeStruct(keys.shape, jnp.float32)
+    return pl.pallas_call(
+        functools.partial(key_back_kernel, head_dim),
+        out_shape=(shape, shape),
+        in_specs=in_vmem(5),
+        out_specs=tuple(in_vmem(2)),
+        scratch_shapes=[pltpu.VMEM((block, width), jnp.float32)],
+        compiler_params=params,
+    )(base, keys, values, query_all, grad_all)
+
+
+def with_stats(rows_t, stats):
+    parts, rest = [], stats
+    for _ in range(3):
+        top = lax.reduce_precision(rest, 8, 7)
+        parts.append(low(top))
+        rest = rest - top
+    parts.append(jnp.zeros((16 - 3 * stats.shape[0], stats.shape[1]), jnp.bfloat16))
+    return jnp.concatenate([rows_t] + parts, axis=0)
 
 
 def f32_dot(spec, left, right):
@@ -276,16 +339,22 @@
     kv_t = low(f32_dot("ck,tc->kt", w_kv, normed1_low))
     kv_all = lax.all_gather(kv_t, "ctx", axis=0)
     query_low = low(f32_dot("tc,ck->tk", normed1_low, w_query))
-    query_t = query_low.T
+    key_low, value_low = kv_t[:head_cols].T, kv_t[head_cols:].T
 
     width = seq_len + block_len
-    window = lax.dynamic_slice_in_dim(
-        jnp.pad(bucket_table, (0, 1)), seq_len - block_len - my_index * block_len, width
-    )
     bucket_ids = jnp.arange(bucket_count, dtype=jnp.int32)
-    in_bucket = (window[None, :] == bucket_ids[:, None]).astype(jnp.float32)
-    line = jnp.einsum("bh,bj->hj", rel_bias, in_bucket, precision=highest)
-    base = jnp.stack([jnp.roll(line, row - (block_len - 1), axis=1) for row in range(8)], axis=1)
+
+    def bias_base(table):
+        window = lax.dynamic_slice_in_dim(
+            jnp.pad(table, (0, 1)), seq_len - block_len - my_index * block_len, width
+        )
+        in_bucket = (window[None, :] == bucket_ids[:, None]).astype(jnp.float32)
+        line = jnp.einsum("bh,bj->hj", rel_bias, in_bucket, precision=highest)
+        rows = [jnp.roll(line, row - (block_len - 1), axis=1) for row in range(8)]
+        return jnp.stack(rows, axis=1), in_bucket
+
+    base, in_bucket = bias_base(bucket_table)
+    base_t, _ = bias_base(bucket_table[::-1])
 
     route_flat = by_sequence(routes).reshape(tok_count)
     expert_ids = jnp.arange(expert_count, dtype=jnp.int32)
@@ -307,6 +376,9 @@
     attended_low = low(attended)
     attn_share = f32_dot("tk,kd->td", attended_low, w_proj)
     attn_out = lax.psum(low(attn_share), "wa").astype(jnp.float32)
+    query_pack = with_stats(query_low.T, lse[:, :, 0])
+    query_pack, attn_out = lax.optimization_barrier((query_pack, attn_out))
+    query_all = lax.all_gather(query_pack, "ctx", axis=0)
     hidden1 = flat_rows + attn_out
     normed2, scale2 = rms_forward(hidden1, gain_ffn)
     normed2_low = low(normed2)
@@ -354,51 +426,51 @@
     grad_attn_low = low(grad_hidden1)
     grad_proj = f32_dot("tk,td->kd", attended_low, grad_attn_low)
     grad_attended = low(f32_dot("td,kd->tk", grad_attn_low, w_proj))
-    dquery, dkv, dline = attend_back(
-        base,
-        query_low,
-        query_t,
-        grad_attended,
-        grad_attended.T,
-        attended,
-        lse,
-        kv_all,
-        head_dim,
-    )
-    dkv_t = lax.psum_scatter(dkv, "ctx", scatter_dimension=0)
+    delta = jnp.sum(
+        (grad_attended.astype(jnp.float32) * attended).reshape(tok_count, head_local, head_dim),
+        axis=2,
+    )
+    grad_all = lax.all_gather(with_stats(grad_attended.T, delta.T), "ctx", axis=0)
+    early = jnp.concatenate(
+        [low(grad_proj), low(grad_router).T, low(grad_gain2)[None, :]], axis=0
+    )
+    dquery, dline = attend_back(
+        base, query_low, grad_attended, attended, lse, kv_all, head_dim
+    )
+    dkey, dvalue = key_back(base_t, key_low, value_low, query_all, grad_all, head_dim)
+    early_sum = lax.psum(early, "ctx")
     folded = sum(jnp.roll(dline[:, row, :], block_len - 1 - row, axis=1) for row in range(8))
     grad_bias = jnp.einsum("bj,hj->bh", in_bucket, folded, precision=highest)
     dquery_low = low(dquery)
-    grad_wq = f32_dot("tc,tk->ck", normed1_low, dquery_low)
-    grad_wkv = f32_dot("tc,kt->ck", normed1_low, dkv_t)
-    grad_normed1_part = f32_dot("tk,ck->tc", dquery_low, w_query) + f32_dot(
-        "kt,ck->tc", dkv_t, w_kv
-    )
+    dqkv_low = jnp.concatenate([dquery_low, low(dkey), low(dvalue)], axis=1)
+    w_qkv = jnp.concatenate([w_query, w_kv], axis=1)
+    grad_wqkv = low(f32_dot("tc,tk->ck", normed1_low, dqkv_low))
+    grad_normed1_part = f32_dot("tk,ck->tc", dqkv_low, w_qkv)
+    gain_part = jnp.sum(grad_normed1_part * flat_rows * scale1, axis=0)
+    small = jnp.concatenate([gain_part, grad_bias.reshape(-1)])
+    small = jnp.pad(small, (0, -small.shape[0] % 1024)).reshape(-1, 128)
+    small_all = lax.all_gather(small, ("ctx", "wa"), axis=0).reshape(ctx_size, wa_size, -1)
+    sum_gain1 = jnp.sum(small_all[:, :, :model_width], axis=(0, 1))
+    bias_all = jnp.sum(small_all[:, :, model_width : model_width + grad_bias.size], axis=0)
+    sum_bias = lax.dynamic_index_in_dim(bias_all, wa_index, 0, False).reshape(grad_bias.shape)
     grad_normed1 = lax.psum(low(grad_normed1_part), "wa").astype(jnp.float32)
-    grad_norm1_in, grad_gain1 = rms_backward(flat_rows, scale1, gain_attn, grad_normed1)
+    grad_norm1_in, _ = rms_backward(flat_rows, scale1, gain_attn, grad_normed1)
     grad_inputs = grad_hidden1 + grad_norm1_in
 
-    def over_ctx(values):
-        return lax.psum(low(values), "ctx").astype(jnp.float32)
-
-    sum_proj = over_ctx(grad_proj)
-    sum_router = over_ctx(grad_router)
-    sum_gain2 = over_ctx(grad_gain2)
-    sum_wq = over_ctx(grad_wq)
-    sum_bias = over_ctx(grad_bias)
-    sum_wkv = over_ctx(grad_wkv)
-    sum_gain1 = over_ctx(grad_gain1)
+    grad_wqkv, early_sum = lax.optimization_barrier((grad_wqkv, early_sum))
+    sum_wqkv = lax.psum(grad_wqkv, "ctx").astype(jnp.float32)
+    early_sum = early_sum.astype(jnp.float32)
     return (
         by_position(output_rows),
         by_position(grad_inputs),
         sum_gain1,
-        sum_wq,
-        sum_wkv[:, :head_cols],
-        sum_wkv[:, head_cols:],
-        sum_proj,
+        sum_wqkv[:, :head_cols],
+        sum_wqkv[:, head_cols : 2 * head_cols],
+        sum_wqkv[:, 2 * head_cols :],
+        early_sum[:head_cols],
         sum_bias,
-        sum_gain2,
-        sum_router,
+        early_sum[head_cols + expert_count],
+        early_sum[head_cols : head_cols + expert_count].T,
         grad_win,
         grad_wout,
     )

time: 533 us -> 592 us (1.11)
  waiting for transfers between devices: 281 us -> 312 us
  local copies, waits for them, and re-layouts: 40.2 us -> 68.8 us
  other arithmetic: 30.6 us -> 22 us
  Pallas kernels: 27.5 us -> 33.8 us
    reduce_scatter x1 -> x0, waiting for transfers between devices: 60.5 us -> none  [body(): dkv_t = lax.psum_scatter(dkv, 'ctx', scatter_dimension=0)]
    psum x1 -> x2, waiting for transfers between devices: 39.7 us -> 84.5 us  [the longest x1 54.3 us: body(): early_sum = lax.psum(early, 'ctx')]
    all_gather x0 -> x1, blocking collectives: none -> 41.3 us  [body(): lax.all_gather(small, ('ctx', 'wa'), axis=0).reshape(ctx_size, wa_size, -1)]
    psum x1 -> x0, blocking collectives: 37.7 us -> none  [over_ctx(): return lax.psum(low(values), 'ctx').astype(jnp.float32)]
    all_gather x0 -> x2, waiting for transfers between devices: none -> 37.5 us  [the longest x1 37.5 us: body(): lax.all_gather(with_stats(grad_attended.T, delta.T), 'ctx', axis=0)]
    all_gather x1, waiting for transfers between devices: 36.8 us -> 50.8 us  [body(): kv_all = lax.all_gather(kv_t, 'ctx', axis=0)]
    pallas_call x0 -> x1, Pallas kernels: none -> 13.5 us  [key_back(): pl.pallas_call(functools.partial(key_back_kernel, head_dim), out_shape=(s...]
    psum x1, waiting for transfers between devices: 23.4 us -> 32.2 us  [body(): grad_normed1 = lax.psum(low(grad_normed1_part), 'wa').astype(jnp.float32)]
  transfers between devices with their start and end apart: 8 -> 10, of which waited for: 8 -> 9; matrix products, arithmetic and copies ran while one was open for 12% -> 16% of each run, Pallas kernels for 0% -> 4%
where the time goes in v2:
time: 592 us; the launch traced here: 584 us
  waiting for transfers between devices  312 us (53%)
  blocking collectives  91.7 us (15%)
  local copies, waits for them, and re-layouts  68.8 us (12%)
  matrix products  38.8 us (7%)
  Pallas kernels  33.8 us (6%)
  other arithmetic  22 us (4%)
  between operations  15.7 us (3%)
    psum x1, waiting for transfers between devices, body(): early_sum = lax.psum(early, 'ctx')  54.3 us
    all_gather x1, waiting for transfers between devices, body(): kv_all = lax.all_gather(kv_t, 'ctx', axis=0)  50.8 us
    all_gather x1, blocking collectives, body(): lax.all_gather(small, ('ctx', 'wa'), axis=0).reshape(ctx_size, wa_size, -1)  41.3 us
    reduce_scatter x1, waiting for transfers between devices, body(): lax.psum_scatter(rows_out, 'wa', scatter_dimension=0, tiled=True)  38.1 us
    all_gather x1, waiting for transfers between devices, body(): lax.all_gather(with_stats(grad_attended.T, delta.T), 'ctx', axis=0)  37.5 us
    dot_general x17, matrix products, f32_dot(): return jnp.einsum(spec, left, right, preferred_element_type=jnp.float32)  35.1 us
    psum x1, waiting for transfers between devices, body(): grad_normed1 = lax.psum(low(grad_normed1_part), 'wa').astype(jnp.float32)  32.2 us
    psum x1, waiting for transfers between devices, body(): sum_wqkv = lax.psum(grad_wqkv, 'ctx').astype(jnp.float32)  30.2 us
  transfers between devices with their start and end apart: 10, of which 9 were waited for; matrix products, arithmetic and copies ran while one was open for 16% of the time, Pallas kernels for 4%

profile of v2, /device:TPU:0, one launch (start us, length us, event | category | flops | bytes accessed | tf_op | source)
XLA Modules:
  0.0 583.6 jit_solution(14666435335767661399)
XLA Ops:
  28.2 50.8 %all-gather.13.cloned.1.call-done = bf16[3072,512]{0,1:T(8,128)(2,1)} async-done(((bf16[384,512]{0,1:T(8,128)(2,1)}), bf16[3072,512]{0,1:T(8,128)(2,1)}) %all-gather.13.cloned.1.call-update) | async-done | bytes 3145744 | tf_op jit(solution)/shard_map/all_gather | solution.py:340
  79.1 4.7 copy.218
  83.7 8.2 %shard_map.229 = (f32[512,192]{1,0:T(8,128)}, f32[3,512,1]{2,1,0:T(8,128)}) custom-call(f32[3,8,2304]{2,1,0:T(8,128)} %stack.62.base_ref, bf16[512,192]{1,0:T(8,128)(2,1)} %convolution_convert_fusion.8.query_ref, bf16[8,384,512]{2,1,0:T(8,128)(2,1)} %bitcast.151), custom_call_target="tpu_custom_call" | custom-call | tf_op jit(solution)/shard_map/pallas_call | solution.py:227
  95.1 2.7 copy.188
  98.4 3.8 copy.187
  105.2 22.0 %all-reduce.8.cloned.1.call-done = bf16[512,768]{1,0:T(8,128)(2,1)} async-done(((bf16[512,768]{1,0:T(8,128)(2,1)}), bf16[512,768]{1,0:T(8,128)(2,1)}) %all-reduce.8.cloned.1.call-update) | async-done | bytes 786448 | tf_op jit(solution)/shard_map/psum | solution.py:378
  132.0 24.7 %all_to_all.24 = bf16[8,32,1536]{2,1,0:T(8,128)(2,1)} all-to-all(bf16[8,32,1536]{2,1,0:T(8,128)(2,1)S(1)} %bitcast.167), channel_id=1, replica_groups=mesh['ctx'=8,'wa'=4] {'ctx'}, dimensions={0} | all-to-all | bytes 1572864 | tf_op jit(solution)/shard_map/all_to_all | solution.py:392
  156.8 27.2 %all-gather.9.cloned.1.call-done = bf16[1024,1536]{1,0:T(8,128)(2,1)} async-done(((bf16[256,1536]{1,0:T(8,128)(2,1)}), bf16[1024,1536]{1,0:T(8,128)(2,1)}) %all-gather.9.cloned.1.call-update) | async-done | bytes 3145744 | tf_op jit(solution)/shard_map/all_gather | solution.py:393
  183.9 3.1 fusion.22
  190.1 3.0 fusion.6
  197.9 38.1 %reduce-scatter.2.cloned.1.call-done = bf16[256,1536]{0,1:T(8,128)(2,1)} async-done(((bf16[1024,1536]{0,1:T(8,128)(2,1)}), bf16[256,1536]{0,1:T(8,128)(2,1)}) %reduce-scatter.2.cloned.1.call-update) | async-done | bytes 786448 | tf_op jit(solution)/shard_map/reduce_scatter | solution.py:405
  237.4 25.7 %all_to_all.25 = bf16[8,32,1536]{2,1,0:T(8,128)(2,1)} all-to-all(bf16[8,32,1536]{2,1,0:T(8,128)(2,1)S(1)} %bitcast.158), channel_id=1, replica_groups=mesh['ctx'=8,'wa'=4] {'ctx'}, dimensions={0} | all-to-all | bytes 1572864 | tf_op jit(solution)/shard_map/all_to_all | solution.py:406
  270.6 19.3 %all-gather.11.cloned.1.call-done = bf16[1024,1536]{1,0:T(8,128)(2,1)} async-done(((bf16[256,1536]{1,0:T(8,128)(2,1)}), bf16[1024,1536]{1,0:T(8,128)(2,1)}) %all-gather.11.cloned.1.call-update) | async-done | bytes 3145744 | tf_op jit(solution)/shard_map/all_gather | solution.py:407
  290.0 3.9 fusion.7
  308.8 4.9 convolution_bitcast_fusion.3
  313.7 3.2 convolution_bitcast_fusion.2
  316.9 12.1 %shard_map.230 = (f32[512,192]{1,0:T(8,128)}, f32[3,8,2304]{2,1,0:T(8,128)}) custom-call(f32[3,8,2304]{2,1,0:T(8,128)} %stack.62.base_ref, bf16[512,192]{1,0:T(8,128)(2,1)} %convolution_convert_fusion.8.query_ref, bf16[512,192]{1,0:T(8,128)(2,1)} %copy-done.14, f32[512,192]{1,0:T(8,128)} %get-tuple-element.23.out_ref, ...), custom_call_target="tpu_custom_call" | custom-call | flops 1207959552 | bytes 40000000 | tf_op jit(solution)/shard_map/pallas_call | solution.py:247
  343.0 3.8 copy.226
  346.7 37.5 %all-gather.17.cloned.1.call-done = bf16[1664,512]{1,0:T(8,128)(2,1)} async-done(((bf16[208,512]{1,0:T(8,128)(2,1)}), bf16[1664,512]{1,0:T(8,128)(2,1)}) %all-gather.17.cloned.1.call-update) | async-done | bytes 1703952 | tf_op jit(solution)/shard_map/all_gather | solution.py:433
  384.3 13.5 %shard_map.231 = (f32[512,192]{1,0:T(8,128)}, f32[512,192]{1,0:T(8,128)}) custom-call(f32[3,8,2304]{2,1,0:T(8,128)} %stack.71.base_ref, bf16[512,192]{1,0:T(8,128)(2,1)} %get-tuple-element.104.key_ref, bf16[512,192]{1,0:T(8,128)(2,1)} %get-tuple-element.103.value_ref, bf16[8,208,512]{2,1,0:T(8,128)(2,1)} %bitcast.161, bf16[8,208,512]{2,1,0:T(8,128)(2,1)} %bitcast.162), custom_call_target="tpu_custom_call" | custom-call | tf_op jit(solution)/shard_map/pallas_call | solution.py:270
  404.1 54.3 %all-reduce.12.cloned.1.call-done = bf16[201,768]{1,0:T(8,128)(2,1)} async-done(((bf16[201,768]{1,0:T(8,128)(2,1)}), bf16[201,768]{1,0:T(8,128)(2,1)}) %all-reduce.12.cloned.1.call-update) | async-done | bytes 308752 | tf_op jit(solution)/shard_map/psum | solution.py:441
  462.5 32.2 %all-reduce.10.cloned.1.call-done = bf16[512,768]{1,0:T(8,128)(2,1)} async-done(((bf16[512,768]{1,0:T(8,128)(2,1)}), bf16[512,768]{1,0:T(8,128)(2,1)}) %all-reduce.10.cloned.1.call-update) | async-done | bytes 786448 | tf_op jit(solution)/shard_map/psum | solution.py:456
  497.0 41.3 %all_gather.35 = f32[32,8,128]{2,1,0:T(8,128)S(1)} all-gather(f32[1,8,128]{2,1,0:T(8,128)S(1)} %fusion.74), channel_id=1, replica_groups=mesh['ctx'=8,'wa'=4] {'ctx','wa'}, dimensions={0}, use_global_device_ids=true | all-gather | bytes 135168 | tf_op jit(solution)/shard_map/all_gather | solution.py:452
  544.0 30.2 %all-reduce.14.cloned.1.call-done = bf16[768,576]{0,1:T(8,128)(2,1)} async-done(((bf16[768,576]{0,1:T(8,128)(2,1)}), bf16[768,576]{0,1:T(8,128)(2,1)}) %all-reduce.14.cloned.1.call-update) | async-done | bytes 884752 | tf_op jit(solution)/shard_map/psum | solution.py:461
  (351 shorter events, 97.6 us)
Async XLA Ops:
  7.2 179.9 %copy-start = (bf16[1,768,768]{2,1,0:T(8,128)(2,1)S(1)}, bf16[1,768,768]{2,1,0:T(8,128)(2,1)}, u32[]{:S(2)}) copy-start(bf16[1,768,768]{2,1,0:T(8,128)(2,1)} %param.25) | copy-start | bytes 3538948
  7.2 71.9 %all-gather.13.cloned.1.call-start = ((), (), s32[]{:S(2)}) async-start(), calls=%async_computation.10 | async-start | bytes 3538944 | tf_op jit(solution)/shard_map/all_gather | solution.py:340
  10.4 15.8 %copy-start.21 = (bf16[512,768]{1,0:T(8,128)(2,1)}, bf16[512,768]{1,0:T(8,128)(2,1)S(1)}, u32[]{:S(2)}) copy-start(bf16[512,768]{1,0:T(8,128)(2,1)S(1)} %multiply_convert_fusion.2) | copy-start | bytes 2359300
  13.1 114.1 %all-reduce.8.cloned.1.call-start = ((), (), s32[]{:S(2)}) async-start(), calls=%async_computation.3 | async-start | bytes 1572864 | tf_op jit(solution)/shard_map/psum | solution.py:378
  94.2 89.7 %all-gather.9.cloned.1.call-start = ((), (), s32[]{:S(2)}) async-start(), calls=%async_computation.4 | async-start | bytes 3932160 | tf_op jit(solution)/shard_map/all_gather | solution.py:393
  103.2 25.2 %copy-start.18 = (bf16[7,512]{0,1:T(8,128)(2,1)}, bf16[7,512]{0,1:T(8,128)(2,1)S(1)}, u32[]{:S(2)}) copy-start(bf16[7,512]{0,1:T(8,128)(2,1)S(1)} %broadcast.205) | copy-start | bytes 21508
  156.7 79.2 %reduce-scatter.2.cloned.1.call-start = ((), (), s32[]{:S(2)}) async-start(), calls=%async_computation.5 | async-start | bytes 3932160 | tf_op jit(solution)/shard_map/reduce_scatter | solution.py:405
  197.8 92.1 %all-gather.11.cloned.1.call-start = ((), (), s32[]{:S(2)}) async-start(), calls=%async_computation.6 | async-start | bytes 3932160 | tf_op jit(solution)/shard_map/all_gather | solution.py:407
  237.3 25.8 %copy-start.62 = (s32[2304]{0:T(1024)S(1)}, s32[2304]{0:T(1024)}, u32[]{:S(2)}) copy-start(s32[2304]{0:T(1024)} %get-tuple-element.125) | copy-start | bytes 27652
  237.4 25.8 %copy-start.80 = (f32[32,3]{0,1:T(4,128)S(1)}, f32[32,3]{0,1:T(4,128)}, u32[]{:S(2)}) copy-start(f32[32,3]{0,1:T(4,128)} %param.21) | copy-start | bytes 1156
  237.4 30.9 %copy-start.20 = (bf16[208,512]{0,1:T(8,128)(2,1)S(1)}, bf16[208,512]{0,1:T(8,128)(2,1)}, u32[]{:S(2)}) copy-start(bf16[208,512]{0,1:T(8,128)(2,1)} %concatenate.125) | copy-start | bytes 638980
  263.1 26.9 %copy-start.73 = (s32[512]{0:T(512)S(1)}, s32[512]{0:T(512)}, u32[]{:S(2)}) copy-start(s32[512]{0:T(512)} %fusion.77) | copy-start | bytes 6148
  263.1 83.6 %all-gather.15.cloned.1.call-start = ((), (), s32[]{:S(2)}) async-start(), calls=%async_computation.11 | async-start | bytes 1916928 | tf_op jit(solution)/shard_map/all_gather | solution.py:381
  263.4 30.4 %copy-start.13 = (f32[3,2304]{1,0:T(4,128)}, f32[3,2304]{1,0:T(4,128)S(1)}, u32[]{:S(2)}) copy-start(f32[3,2304]{1,0:T(4,128)S(1)} %convolution_bitcast_fusion) | copy-start | bytes 82948
  269.1 115.1 %all-gather.17.cloned.1.call-start = ((), (), s32[]{:S(2)}) async-start(), calls=%async_computation.12 | async-start | bytes 1916928 | tf_op jit(solution)/shard_map/all_gather | solution.py:433
  270.6 23.2 %copy-start.33 = (f32[512]{0:T(512)S(1)}, f32[512]{0:T(512)}, u32[]{:S(2)}) copy-start(f32[512]{0:T(512)} %copy-done.32) | copy-start | bytes 6148
  305.5 153.0 %all-reduce.12.cloned.1.call-start = ((), (), s32[]{:S(2)}) async-start(), calls=%async_computation.8 | async-start | bytes 638976 | tf_op jit(solution)/shard_map/psum | solution.py:441
  329.0 11.5 %copy-start.34 = (f32[512]{0:T(512)S(1)}, f32[512]{0:T(512)}, u32[]{:S(2)}) copy-start(f32[512]{0:T(512)} %copy-done.32) | copy-start | bytes 6148
  342.2 152.5 %all-reduce.10.cloned.1.call-start = ((), (), s32[]{:S(2)}) async-start(), calls=%async_computation.7 | async-start | bytes 1572864 | tf_op jit(solution)/shard_map/psum | solution.py:456
  402.3 171.9 %all-reduce.14.cloned.1.call-start = ((), (), s32[]{:S(2)}) async-start(), calls=%async_computation.9 | async-start | bytes 1769472 | tf_op jit(solution)/shard_map/psum | solution.py:461
  404.1 90.6 %copy-start.40 = (f32[768]{0:T(1024)S(1)}, f32[768]{0:T(1024)}, u32[]{:S(2)}) copy-start(f32[768]{0:T(1024)} %param.16) | copy-start | bytes 9220
  404.1 90.6 %copy-start.55 = (f32[1,2,2,128]{3,1,2,0:T(2,128)S(1)}, f32[1,2,2,128]{3,1,2,0:T(2,128)}, u32[]{:S(2)}) copy-start(f32[1,2,2,128]{3,1,2,0:T(2,128)} %copy-done.54) | copy-start | bytes 6148
  494.8 44.3 %copy-start.12 = (bf16[512,768]{1,0:T(8,128)(2,1)S(1)}, bf16[512,768]{1,0:T(8,128)(2,1)}, u32[]{:S(2)}) copy-start(bf16[512,768]{1,0:T(8,128)(2,1)} %all-reduce.10.cloned.1.call-done) | copy-start | bytes 2359300
  543.4 33.2 %copy-start.1 = (bf16[1,768,768]{2,1,0:T(8,128)(2,1)S(1)}, bf16[1,768,768]{2,1,0:T(8,128)(2,1)}, u32[]{:S(2)}) copy-start(bf16[1,768,768]{2,1,0:T(8,128)(2,1)} %param.25) | copy-start | bytes 3538948
  (72 other events, 242.6 us)
Sparse Core Ops, SparseCore 0:
  13.3 65.7 all-gather.12
  94.4 32.7 all-reduce.7
  156.8 27.0 all-gather.8
  197.9 37.9 reduce-scatter.1
  263.2 26.6 all-gather.10
  292.2 45.2 all-gather.14
  340.0 44.2 all-gather.16
  388.6 69.8 all-reduce.11
  460.8 33.8 all-reduce.9
  498.1 76.0 all-reduce.13
